TPU v7x, 512 devices: a whole 4x8x8 slice. The times are simulated.
512 devices in a mesh: vv: 128 (over y, z, core), oo: 4 (over x).
Axes of the slice: x: 4, y: 8, z: 8, core: 2. Of those that a mesh axis runs over, the one named last changes fastest.
Arguments:
- amplitudes: float32 [128, 4, 128, 4096], P(None, 'oo', 'vv'), may hold values from -6 to 6
- tile_len: int32 [16], replicated, may hold values from 40 to 64, as said below
- pair_tiles: int32 [128, 2], P('vv'), may hold values from 0 to 15
- v_blocks: float32 [128, 4, 40, 4096], P('vv'), may hold values from -0.09375 to 0.09375
- block_count: int32 [128], P('vv'), may hold values from 1 to 4, as said below
Outputs:
- ladder: float32 [128, 40, 4, 128], P('vv', None, 'oo')
Inputs may be any that keep to these rules, and one draw needn't show every extreme that they name: `tile_len`: some tile is full. `block_count`: some cd tile pair has all 4 slots live.
All inputs are finite; a program needn't handle non-finite values.
Results may differ from a plain program's by a relative error of at most 0.0003.
Values sent between devices are 32-bit elements; how exact they have to be, the bound alone decides.
No kernel may reach another device: no remote copies, remote signals or barrier semaphores. Data moves between devices by JAX's collectives and lax.ppermute only.
A program may use at most 64 MiB of HBM per device.

v0:
```python
import jax
import jax.numpy as jnp
from jax import lax
from jax.sharding import PartitionSpec as P

TV = 64


def from_behind(block, axis, distance):
    devices = range(lax.axis_size(axis))
    route = [((i - distance) % len(devices), i) for i in devices]
    return lax.ppermute(block, axis, route)


def pair_mask(tile_len, pair_row):
    tiles = jnp.arange(tile_len.shape[0], dtype=jnp.int32)
    c_length = jnp.sum(jnp.where(tiles == pair_row[0], tile_len, 0))
    d_length = jnp.sum(jnp.where(tiles == pair_row[1], tile_len, 0))
    pair_index = jnp.arange(TV * TV, dtype=jnp.int32)
    return ((pair_index // TV < c_length) & (pair_index % TV < d_length)).astype(jnp.float32)


def shards(amplitudes, tile_len, pair_tiles, v_blocks, block_count):
    highest = lax.Precision.HIGHEST
    arrived = lax.all_to_all(amplitudes, "vv", split_axis=0, concat_axis=2, tiled=True)
    row_o = arrived.shape[1]
    row_v = arrived.shape[2]
    cd_mask = pair_mask(tile_len, pair_tiles[0])
    amp_rows = (arrived[0] * cd_mask).reshape(row_o * row_v, TV * TV)
    blocks = v_blocks[0]
    slots = blocks.shape[0]
    window = blocks.shape[1]
    live_count = block_count[0]
    slot_ids = jnp.arange(slots, dtype=jnp.int32)
    live_slots = slot_ids < live_count
    live_weight = live_slots.astype(jnp.float32)

    def add_block(slot, gathered):
        block = lax.dynamic_index_in_dim(blocks, slot, 0, keepdims=False)
        term = lax.dot_general(block, amp_rows, (((1,), (1,)), ((), ())), precision=highest)
        return lax.dynamic_update_index_in_dim(gathered, term, slot, 0)

    products = lax.fori_loop(
        0, live_count, add_block, jnp.zeros((slots, window, amp_rows.shape[0]), jnp.float32)
    )
    owners = lax.axis_size("vv")
    stride = owners // slots
    total = products[0] * live_weight[0]
    for slot in range(1, slots):
        moved = from_behind(products[slot] * live_weight[slot], "vv", slot * stride)
        total = total + moved
    summed = total[None]
    return summed.reshape(1, window, row_o, row_v)


def solution(mesh):
    return jax.shard_map(
        shards,
        mesh=mesh,
        in_specs=(
            P(None, "oo", "vv", None),
            P(),
            P("vv", None),
            P("vv", None, None, None),
            P("vv"),
        ),
        out_specs=P("vv", None, "oo", None),
        check_vma=False,
    )
```

profile of v0, /device:TPU:74, one launch (start us, length us, event | category | flops | bytes accessed | tf_op | source)
XLA Modules:
  0.0 108.0 jit_solution(16567888110784296016)
XLA Ops:
  0.0 0.0 copy-start
  0.0 0.0 copy-start.1
  0.0 17.1 %all-to-all-start = ((f32[128,1,1,4096]{3,2,1,0:T(1,128)}), f32[128,1,1,4096]{3,2,1,0:T(1,128)}, u32[]{:S(2)}, u32[]{:S(2)}) async-start(f32[128,1,1,4096]{3,2,1,0:T(1,128)} %param.7), calls=%async_computation | async-start | bytes 4194304 | tf_op jit(solution)/shard_map/all_to_all | solution.py:25
  17.7 0.0 copy-done
  17.7 0.6 fusion.20
  18.4 0.7 fusion.19
  19.0 0.0 copy-done.1
  19.0 2.0 %fusion.17 = (s32[]{:T(128)}, s32[]{:T(128)}) fusion(s32[16]{0:T(128)S(1)} %copy-done.1, s32[]{:T(128)} %bitcast.4, s32[]{:T(128)} %bitcast.5), kind=kLoop, calls=%fused_computation.30 | loop fusion | flops 94 | bytes 80 | tf_op jit(solution)/shard_map/reduce_sum | solution.py:17
  21.1 1.2 %fusion.16 = f32[4096]{0:T(1024)S(1)} fusion(s32[]{:T(128)} %get-tuple-element.35, s32[]{:T(128)} %get-tuple-element.34), kind=kLoop, calls=%fused_computation.26 | loop fusion | flops 65536 | bytes 16392 | tf_op jit(solution)/shard_map/convert_element_type | solution.py:20
  22.2 47.4 %all-to-all-done = f32[128,1,1,4096]{3,2,1,0:T(1,128)} async-done(((f32[128,1,1,4096]{3,2,1,0:T(1,128)}), f32[128,1,1,4096]{3,2,1,0:T(1,128)}, u32[]{:S(2)}, u32[]{:S(2)}) %all-to-all-start) | async-done | bytes 2097184 | tf_op jit(solution)/shard_map/all_to_all | solution.py:25
  69.6 3.3 %bitcast_multiply_fusion = f32[128,4096]{1,0:T(8,128)S(1)} fusion(f32[128,1,1,4096]{3,2,1,0:T(1,128)} %all-to-all-done, f32[4096]{0:T(1024)S(1)} %fusion.16), kind=kLoop, calls=%fused_computation.5 | loop fusion | flops 524288 | bytes 4210688 | tf_op jit(solution)/shard_map/mul | solution.py:29
  72.9 4.6 %while.10 = (s32[]{:T(128)}, f32[4,40,128]{2,1,0:T(8,128)S(1)}, s32[]{:T(128)}, f32[4,40,4096]{2,1,0:T(8,128)}, f32[128,4096]{1,0:T(8,128)S(1)}, /*index=5*/s32[]{:T(128)}, s32[]{:T(128)}, s32[]{:T(128)}) while((s32[]{:T(128)}, f32[4,40,128]{2,1,0:T(8,128)S(1)}, s32[]{:T(128)}, f32[4,40,4096]{2,1,0:T(8,128)}, f32[128,4096]{1,0:T(8,128)S(1)}, ...), condition=%wide.region_3.4_spmd, body=%wide.region_2.3_spmd.sunk | while | flops 251658240 | bytes 2774135 | solution.py:43
  73.6 3.3 %fusion.27 = f32[4,40,128]{2,1,0:T(8,128)S(1)} fusion(f32[4,40,128]{2,1,0:T(8,128)S(1)} %get-tuple-element.96, s32[]{:T(128)S(6)} %select_n.56, f32[128,4096]{1,0:T(8,128)S(1)} %get-tuple-element.107, f32[4,40,4096]{2,1,0:T(8,128)} %get-tuple-element.106), kind=kOutput, calls=%fused_computation.1.clone.1 | convolution fusion | flops 251658240 | bytes 2774016 | tf_op jit(solution)/shard_map/while/body/dot_general | solution.py:40
  77.5 1.9 %multiply_bitcast_fusion.2 = (f32[40,128]{1,0:T(8,128)S(1)}, f32[40,128]{1,0:T(8,128)S(1)}, f32[40,128]{1,0:T(8,128)S(1)}) fusion(f32[4,40,128]{2,1,0:T(8,128)S(1)} %get-tuple-element.33, f32[]{:T(128)} %bitcast.8, f32[]{:T(128)} %bitcast.12, f32[]{:T(128)} %bitcast.10), kind=kLoop, calls=%fused_computation.19 | loop fusion | flops 15360 | bytes 122892 | tf_op jit(solution)/shard_map/mul | solution.py:50
  79.5 13.4 %collective-permute-start = (f32[40,128]{1,0:T(8,128)S(1)}, f32[40,128]{1,0:T(8,128)S(1)}, u32[]{:S(2)}, u32[]{:S(2)}) collective-permute-start(f32[40,128]{1,0:T(8,128)S(1)} %get-tuple-element.46), channel_id=1, source_target_pairs={{384,0},{388,4},{392,8},{396,12},{400,16},{404,20},{408,24},{412,2... | collective-permute-start | bytes 61448 | tf_op jit(solution)/shard_map/ppermute | solution.py:12
  92.9 7.3 %collective-permute-start.1 = (f32[40,128]{1,0:T(8,128)S(1)}, f32[40,128]{1,0:T(8,128)S(1)}, u32[]{:S(2)}, u32[]{:S(2)}) collective-permute-start(f32[40,128]{1,0:T(8,128)S(1)} %get-tuple-element.48), channel_id=1, source_target_pairs={{256,0},{260,4},{264,8},{268,12},{272,16},{276,20},{280,24},{284,2... | collective-permute-start | bytes 61448 | tf_op jit(solution)/shard_map/ppermute | solution.py:12
  100.1 3.6 %collective-permute-start.2 = (f32[40,128]{1,0:T(8,128)S(1)}, f32[40,128]{1,0:T(8,128)S(1)}, u32[]{:S(2)}, u32[]{:S(2)}) collective-permute-start(f32[40,128]{1,0:T(8,128)S(1)} %get-tuple-element.47), channel_id=1, source_target_pairs={{128,0},{132,4},{136,8},{140,12},{144,16},{148,20},{152,24},{156,2... | collective-permute-start | bytes 61448 | tf_op jit(solution)/shard_map/ppermute | solution.py:12
  103.7 0.0 collective-permute-done
  103.7 0.0 collective-permute-done.1
  103.7 3.0 %collective-permute-done.2 = f32[40,128]{1,0:T(8,128)S(1)} collective-permute-done((f32[40,128]{1,0:T(8,128)S(1)}, f32[40,128]{1,0:T(8,128)S(1)}, u32[]{:S(2)}, u32[]{:S(2)}) %collective-permute-start.2) | collective-permute-done | bytes 20512 | tf_op jit(solution)/shard_map/ppermute | solution.py:12
  106.7 1.3 %fusion.9 = f32[40,128]{1,0:T(8,128)} fusion(f32[40,128]{1,0:T(8,128)S(1)} %collective-permute-done.2, f32[40,128]{1,0:T(8,128)S(1)} %collective-permute-done.1, f32[40,128]{1,0:T(8,128)S(1)} %collective-permute-done, f32[4,40,128]{2,1,0:T(8,128)S(1)} %get-tuple-element.33, f32[]{:T(128)} %bitcast.6), kind=kLoop, calls=%fused_computation.16 | loop fusion | flops 20480 | bytes 102404 | tf_op jit(solution)/shard_map/add | solution.py:51
  (2 shorter events, 0.0 us)
Async XLA Ops:
  0.0 17.7 %copy-start = (s32[1,2]{1,0:T(1,128)S(1)}, s32[1,2]{1,0:T(1,128)}, u32[]{:S(2)}) copy-start(s32[1,2]{1,0:T(1,128)} %param.9) | copy-start | bytes 28
  0.0 19.0 %copy-start.1 = (s32[16]{0:T(128)S(1)}, s32[16]{0:T(128)}, u32[]{:S(2)}) copy-start(s32[16]{0:T(128)} %param.8) | copy-start | bytes 196
  0.0 69.6 %all-to-all-start = ((f32[128,1,1,4096]{3,2,1,0:T(1,128)}), f32[128,1,1,4096]{3,2,1,0:T(1,128)}, u32[]{:S(2)}, u32[]{:S(2)}) async-start(f32[128,1,1,4096]{3,2,1,0:T(1,128)} %param.7), calls=%async_computation | async-start | bytes 4194304 | tf_op jit(solution)/shard_map/all_to_all | solution.py:25
  79.5 24.3 %collective-permute-start = (f32[40,128]{1,0:T(8,128)S(1)}, f32[40,128]{1,0:T(8,128)S(1)}, u32[]{:S(2)}, u32[]{:S(2)}) collective-permute-start(f32[40,128]{1,0:T(8,128)S(1)} %get-tuple-element.46), channel_id=1, source_target_pairs={{384,0},{388,4},{392,8},{396,12},{400,16},{404,20},{408,24},{412,2... | collective-permute-start | bytes 61448 | tf_op jit(solution)/shard_map/ppermute | solution.py:12
  92.9 10.9 %collective-permute-start.1 = (f32[40,128]{1,0:T(8,128)S(1)}, f32[40,128]{1,0:T(8,128)S(1)}, u32[]{:S(2)}, u32[]{:S(2)}) collective-permute-start(f32[40,128]{1,0:T(8,128)S(1)} %get-tuple-element.48), channel_id=1, source_target_pairs={{256,0},{260,4},{264,8},{268,12},{272,16},{276,20},{280,24},{284,2... | collective-permute-start | bytes 61448 | tf_op jit(solution)/shard_map/ppermute | solution.py:12
  100.1 6.6 %collective-permute-start.2 = (f32[40,128]{1,0:T(8,128)S(1)}, f32[40,128]{1,0:T(8,128)S(1)}, u32[]{:S(2)}, u32[]{:S(2)}) collective-permute-start(f32[40,128]{1,0:T(8,128)S(1)} %get-tuple-element.47), channel_id=1, source_target_pairs={{128,0},{132,4},{136,8},{140,12},{144,16},{148,20},{152,24},{156,2... | collective-permute-start | bytes 61448 | tf_op jit(solution)/shard_map/ppermute | solution.py:12
where the time goes:
time: 109 us; the launch traced here: 108 us
  waiting for transfers between devices  50.4 us (46%)
  starting transfers between devices  41.3 us (38%)
  other arithmetic  9.68 us (9%)
  matrix products  3.3 us (3%)
  local copies, waits for them, and re-layouts  1.32 us (1%)
  loops' own time  1.32 us (1%)
    all_to_all x1, waiting for transfers between devices, shards(): lax.all_to_all(amplitudes, 'vv', split_axis=0, concat_axis=2, tiled=True)  47.4 us
    ppermute x3, starting transfers between devices, from_behind(): return lax.ppermute(block, axis, route)  24.2 us
    all_to_all x1, starting transfers between devices, shards(): lax.all_to_all(amplitudes, 'vv', split_axis=0, concat_axis=2, tiled=True)  17.1 us
    dot_general x1, matrix products, add_block(): lax.dot_general(block, amp_rows, (((1,), (1,)), ((), ())), precision=high...  3.3 us
    mul x1, other arithmetic, shards(): amp_rows = (arrived[0] * cd_mask).reshape(row_o * row_v, TV * TV)  3.26 us
    ppermute x3, waiting for transfers between devices, from_behind(): return lax.ppermute(block, axis, route)  2.98 us
  transfers between devices with their start and end apart: 4, of which 2 were waited for; matrix products, arithmetic and copies ran while one was open for 4% of the time, Pallas kernels for 0%

commit v1 on v0

v1 whole, which is shorter than its diff:
```python
import jax
import jax.numpy as jnp
from jax import lax
from jax.experimental import pallas as pl
from jax.experimental.pallas import tpu as pltpu
from jax.sharding import PartitionSpec as P

TV = 64
LANES = 128


def split_blocks(tile_len_ref, pair_ref, count_ref, member_ref, v_ref, out_ref):
    slots, window, width = v_ref.shape
    rows = slots * window
    c_length = tile_len_ref[pair_ref[0, 0]]
    d_length = tile_len_ref[pair_ref[0, 1]]
    count = count_ref[0]
    member = member_ref[0]
    step = 4 * LANES
    for start in range(0, width, step):
        lanes = pl.ds(start, step)
        index = lax.broadcasted_iota(jnp.int32, (window, step), 1) + start
        inside = (index // TV < c_length) & (index % TV < d_length)
        blocks = []
        for target in range(slots):
            slot = lax.rem(target - member + slots, slots)
            live = jnp.where(slot < count, 1, 0)
            blocks.append(jnp.where(inside & (live > 0), v_ref[slot, :, lanes], 0.0))
        block = jnp.concatenate(blocks, axis=0)
        head = block.astype(jnp.bfloat16)
        out_ref[0:rows, lanes] = head
        out_ref[rows : 2 * rows, lanes] = (block - head.astype(jnp.float32)).astype(jnp.bfloat16)


def contract(v_ref, amp_ref, out_ref, split_ref):
    rows = out_ref.shape[1]
    depth = amp_ref.shape[0] // rows
    for j in range(depth):
        part = amp_ref[pl.ds(j, rows, stride=depth), :]
        head = part.astype(jnp.bfloat16)
        tail = (part - head.astype(jnp.float32)).astype(jnp.bfloat16)
        lanes = pl.ds(j * LANES, LANES)
        split_ref[0:rows, lanes] = head
        split_ref[rows : 2 * rows, lanes] = tail
    both = lax.dot_general(
        v_ref[...], split_ref[...], (((1,), (1,)), ((), ())), preferred_element_type=jnp.float32
    )
    half = out_ref.shape[0]
    out_ref[...] = (both[half:, rows:] + both[half:, :rows] + both[:half, rows:]) + both[:half, :rows]


def shards(amplitudes, tile_len, pair_tiles, v_blocks, block_count):
    owners = lax.axis_size("vv")
    slots, window, width = v_blocks.shape[1:]
    stride = owners // slots
    depth = width // LANES
    rows = amplitudes.shape[0]
    arrived = lax.all_to_all(
        amplitudes.reshape(rows, depth, LANES), "vv", split_axis=0, concat_axis=0, tiled=True
    )

    member = lax.axis_index("vv") // stride
    v_split = pl.pallas_call(
        split_blocks,
        out_shape=jax.ShapeDtypeStruct((2 * slots * window, width), jnp.bfloat16),
        in_specs=[pl.BlockSpec(memory_space=pltpu.SMEM)] * 4 + [pl.BlockSpec(memory_space=pltpu.VMEM)],
        out_specs=pl.BlockSpec(memory_space=pltpu.VMEM),
        compiler_params=pltpu.CompilerParams(vmem_limit_bytes=24 * 1024 * 1024),
        cost_estimate=pl.CostEstimate(
            flops=8 * slots * window * width, bytes_accessed=8 * slots * window * width, transcendentals=0
        ),
        name="split_blocks",
    )(tile_len, pair_tiles, block_count, member.astype(jnp.int32)[None], v_blocks[0])

    terms = pl.pallas_call(
        contract,
        out_shape=jax.ShapeDtypeStruct((slots * window, rows), jnp.float32),
        in_specs=[pl.BlockSpec(memory_space=pltpu.VMEM)] * 2,
        out_specs=pl.BlockSpec(memory_space=pltpu.VMEM),
        scratch_shapes=[pltpu.VMEM((2 * rows, width), jnp.bfloat16)],
        compiler_params=pltpu.CompilerParams(vmem_limit_bytes=32 * 1024 * 1024),
        cost_estimate=pl.CostEstimate(
            flops=8 * slots * window * rows * width, bytes_accessed=6 * rows * width, transcendentals=0
        ),
        name="contract",
    )(v_split, arrived.reshape(rows * depth, LANES))

    groups = [[i + stride * k for k in range(slots)] for i in range(stride)]
    moved = lax.all_to_all(
        terms.reshape(slots, window, rows), "vv", split_axis=0, concat_axis=0, axis_index_groups=groups, tiled=True
    )
    total = (moved[0] + moved[1]) + (moved[2] + moved[3])
    return total.reshape(1, window, 1, rows)


def solution(mesh):
    return jax.shard_map(
        shards,
        mesh=mesh,
        in_specs=(
            P(None, "oo", "vv", None),
            P(),
            P("vv", None),
            P("vv", None, None, None),
            P("vv"),
        ),
        out_specs=P("vv", None, "oo", None),
        check_vma=False,
    )
```

time: 109 us -> 86.7 us (0.80)
  the two profiles are of different devices: /device:TPU:74 before, /device:TPU:6 now
where the time goes in v1:
time: 86.7 us; the launch traced here: 86 us
  waiting for transfers between devices  48 us (55%)
  starting transfers between devices  18.5 us (21%)
  blocking collectives  11.7 us (13%)
  Pallas kernels  4.73 us (5%)
  local copies, waits for them, and re-layouts  1.74 us (2%)
    all_to_all x1, waiting for transfers between devices, shards(): lax.all_to_all(amplitudes.reshape(rows, depth, LANES), 'vv', split_axis=0...  48 us
    all_to_all x1, starting transfers between devices, shards(): lax.all_to_all(amplitudes.reshape(rows, depth, LANES), 'vv', split_axis=0...  18.5 us
    all_to_all x1, blocking collectives, shards(): lax.all_to_all(terms.reshape(slots, window, rows), 'vv', split_axis=0, co...  11.7 us
    pallas_call x1, Pallas kernels, shards(): pl.pallas_call(contract, out_shape=jax.ShapeDtypeStruct((slots * window,...  3.68 us
    unnamed x6, local copies, waits for them, and re-layouts  1.74 us
  transfers between devices with their start and end apart: 1, of which 1 were waited for; matrix products, arithmetic and copies ran while one was open for 0% of the time, Pallas kernels for 1%

profile of v1, /device:TPU:6, one launch (start us, length us, event | category | flops | bytes accessed | tf_op | source)
XLA Modules:
  0.0 86.0 jit_solution(3775023493339085648)
XLA Ops:
  0.0 0.0 copy-start.2
  0.0 0.0 copy-start.1
  0.0 18.5 %all-to-all-start = ((f32[128,32,128]{2,1,0:T(8,128)}), f32[128,32,128]{2,1,0:T(8,128)}, u32[]{:S(2)}, u32[]{:S(2)}) async-start(f32[128,32,128]{2,1,0:T(8,128)} %bitcast.8), calls=%async_computation | async-start | bytes 4194304 | tf_op jit(solution)/shard_map/all_to_all | solution.py:58
  19.1 0.0 copy-done.2
  19.2 0.0 copy-done.1
  19.2 0.0 copy-start
  19.2 1.7 %copy-done = f32[1,4,40,4096]{3,2,1,0:T(8,128)S(1)} copy-done((f32[1,4,40,4096]{3,2,1,0:T(8,128)S(1)}, f32[1,4,40,4096]{3,2,1,0:T(8,128)}, u32[]{:S(2)}) %copy-start) | copy-done | bytes 2621464
  20.9 1.1 %split_blocks.1.v_ref = bf16[320,4096]{1,0:T(8,128)(2,1)S(1)} custom-call(s32[16]{0:T(128)S(1)} %copy-done.1, s32[1,2]{1,0:T(1,128)S(1)} %copy-done.2, s32[1]{0:T(128)S(6)} %copy.6.count_ref, s32[1]{0:T(128)} %bitcast.member_ref, f32[4,40,4096]{2,1,0:T(8,128)S(1)} %bitcast.6), custom_call_target="tpu_custom_call" | custom-call | flops 5242880 | bytes 5242880 | tf_op jit(solution)/shard_map/split_blocks/pallas_call | solution.py:63
  22.0 48.0 %all-to-all-done = f32[128,32,128]{2,1,0:T(8,128)} async-done(((f32[128,32,128]{2,1,0:T(8,128)}), f32[128,32,128]{2,1,0:T(8,128)}, u32[]{:S(2)}, u32[]{:S(2)}) %all-to-all-start) | async-done | bytes 2097184 | tf_op jit(solution)/shard_map/all_to_all | solution.py:58
  70.0 3.7 %contract.1 = f32[160,128]{1,0:T(8,128)S(1)} custom-call(bf16[320,4096]{1,0:T(8,128)(2,1)S(1)} %split_blocks.1.v_ref, f32[4096,128]{1,0:T(8,128)} %bitcast.3.amp_ref), custom_call_target="tpu_custom_call" | custom-call | flops 671088640 | bytes 3145728 | tf_op jit(solution)/shard_map/contract/pallas_call | solution.py:75
  73.7 11.7 %all_to_all.10 = f32[4,40,128]{2,1,0:T(8,128)S(1)} all-to-all(f32[4,40,128]{2,1,0:T(8,128)S(1)} %bitcast.7), channel_id=1, replica_groups={{0,128,256,384},{4,132,260,388},{8,136,264,392},{12,140,268,396},{16,14..., dimensions={0} | all-to-all | bytes 163840 | tf_op jit(solution)/shard_map/all_to_all | solution.py:89
  85.4 0.6 fusion
Async XLA Ops:
  0.0 19.1 %copy-start.2 = (s32[1,2]{1,0:T(1,128)S(1)}, s32[1,2]{1,0:T(1,128)}, u32[]{:S(2)}) copy-start(s32[1,2]{1,0:T(1,128)} %pair_ref.1) | copy-start | bytes 28
  0.0 19.2 %copy-start.1 = (s32[16]{0:T(128)S(1)}, s32[16]{0:T(128)}, u32[]{:S(2)}) copy-start(s32[16]{0:T(128)} %tile_len_ref.1) | copy-start | bytes 196
  0.0 70.0 %all-to-all-start = ((f32[128,32,128]{2,1,0:T(8,128)}), f32[128,32,128]{2,1,0:T(8,128)}, u32[]{:S(2)}, u32[]{:S(2)}) async-start(f32[128,32,128]{2,1,0:T(8,128)} %bitcast.8), calls=%async_computation | async-start | bytes 4194304 | tf_op jit(solution)/shard_map/all_to_all | solution.py:58
  19.2 1.7 %copy-start = (f32[1,4,40,4096]{3,2,1,0:T(8,128)S(1)}, f32[1,4,40,4096]{3,2,1,0:T(8,128)}, u32[]{:S(2)}) copy-start(f32[1,4,40,4096]{3,2,1,0:T(8,128)} %param.8) | copy-start | bytes 7864324

commit v2 on v1

--- a/solution.py
+++ b/solution.py
@@ -9,9 +9,8 @@
 LANES = 128
 
 
-def split_blocks(tile_len_ref, pair_ref, count_ref, member_ref, v_ref, out_ref):
+def split_blocks(tile_len_ref, pair_ref, count_ref, member_ref, v_ref, head_ref, tail_ref):
     slots, window, width = v_ref.shape
-    rows = slots * window
     c_length = tile_len_ref[pair_ref[0, 0]]
     d_length = tile_len_ref[pair_ref[0, 1]]
     count = count_ref[0]
@@ -28,11 +27,17 @@
             blocks.append(jnp.where(inside & (live > 0), v_ref[slot, :, lanes], 0.0))
         block = jnp.concatenate(blocks, axis=0)
         head = block.astype(jnp.bfloat16)
-        out_ref[0:rows, lanes] = head
-        out_ref[rows : 2 * rows, lanes] = (block - head.astype(jnp.float32)).astype(jnp.bfloat16)
+        head_ref[:, lanes] = head
+        tail_ref[:, lanes] = (block - head.astype(jnp.float32)).astype(jnp.bfloat16)
 
 
-def contract(v_ref, amp_ref, out_ref, split_ref):
+def times_transposed(a, b):
+    return lax.dot_general(a, b, (((1,), (1,)), ((), ())), preferred_element_type=jnp.float32)
+
+
+def contract(head_ref, tail_hbm, amp_ref, out_ref, tail_ref, split_ref, sem):
+    copy = pltpu.make_async_copy(tail_hbm, tail_ref, sem)
+    copy.start()
     rows = out_ref.shape[1]
     depth = amp_ref.shape[0] // rows
     for j in range(depth):
@@ -42,11 +47,10 @@
         lanes = pl.ds(j * LANES, LANES)
         split_ref[0:rows, lanes] = head
         split_ref[rows : 2 * rows, lanes] = tail
-    both = lax.dot_general(
-        v_ref[...], split_ref[...], (((1,), (1,)), ((), ())), preferred_element_type=jnp.float32
-    )
-    half = out_ref.shape[0]
-    out_ref[...] = (both[half:, rows:] + both[half:, :rows] + both[:half, rows:]) + both[:half, :rows]
+    upper = times_transposed(head_ref[...], split_ref[...])
+    copy.wait()
+    lower = times_transposed(tail_ref[...], split_ref[...])
+    out_ref[...] = (lower[:, rows:] + lower[:, :rows] + upper[:, rows:]) + upper[:, :rows]
 
 
 def shards(amplitudes, tile_len, pair_tiles, v_blocks, block_count):
@@ -60,12 +64,15 @@
     )
 
     member = lax.axis_index("vv") // stride
-    v_split = pl.pallas_call(
+    heads, tails = pl.pallas_call(
         split_blocks,
-        out_shape=jax.ShapeDtypeStruct((2 * slots * window, width), jnp.bfloat16),
+        out_shape=[
+            jax.ShapeDtypeStruct((slots * window, width), jnp.bfloat16),
+            pltpu.HBM((slots * window, width), jnp.bfloat16),
+        ],
         in_specs=[pl.BlockSpec(memory_space=pltpu.SMEM)] * 4 + [pl.BlockSpec(memory_space=pltpu.VMEM)],
-        out_specs=pl.BlockSpec(memory_space=pltpu.VMEM),
-        compiler_params=pltpu.CompilerParams(vmem_limit_bytes=24 * 1024 * 1024),
+        out_specs=[pl.BlockSpec(memory_space=pltpu.VMEM)] * 2,
+        compiler_params=pltpu.CompilerParams(vmem_limit_bytes=16 * 1024 * 1024),
         cost_estimate=pl.CostEstimate(
             flops=8 * slots * window * width, bytes_accessed=8 * slots * window * width, transcendentals=0
         ),
@@ -75,15 +82,23 @@
     terms = pl.pallas_call(
         contract,
         out_shape=jax.ShapeDtypeStruct((slots * window, rows), jnp.float32),
-        in_specs=[pl.BlockSpec(memory_space=pltpu.VMEM)] * 2,
+        in_specs=[
+            pl.BlockSpec(memory_space=pltpu.VMEM),
+            pl.BlockSpec(memory_space=pl.ANY),
+            pl.BlockSpec(memory_space=pltpu.VMEM),
+        ],
         out_specs=pl.BlockSpec(memory_space=pltpu.VMEM),
-        scratch_shapes=[pltpu.VMEM((2 * rows, width), jnp.bfloat16)],
-        compiler_params=pltpu.CompilerParams(vmem_limit_bytes=32 * 1024 * 1024),
+        scratch_shapes=[
+            pltpu.VMEM((slots * window, width), jnp.bfloat16),
+            pltpu.VMEM((2 * rows, width), jnp.bfloat16),
+            pltpu.SemaphoreType.DMA,
+        ],
+        compiler_params=pltpu.CompilerParams(vmem_limit_bytes=16 * 1024 * 1024),
         cost_estimate=pl.CostEstimate(
             flops=8 * slots * window * rows * width, bytes_accessed=6 * rows * width, transcendentals=0
         ),
         name="contract",
-    )(v_split, arrived.reshape(rows * depth, LANES))
+    )(heads, pltpu.with_memory_space_constraint(tails, pltpu.HBM), arrived.reshape(rows * depth, LANES))
 
     groups = [[i + stride * k for k in range(slots)] for i in range(stride)]
     moved = lax.all_to_all(

time: 86.7 us -> 85.9 us (level)
    pallas_call x1, Pallas kernels: 1.06 us -> 1.99 us  [shards(): pl.pallas_call(split_blocks, out_shape=[jax.ShapeDtypeStruct((slots * win...]
  transfers between devices with their start and end apart: 1 -> 1, of which waited for: 1 -> 1; matrix products, arithmetic and copies ran while one was open for 0% -> 0% of each run, Pallas kernels for 1% -> 2%
where the time goes in v2:
time: 85.9 us; the launch traced here: 85.6 us
  waiting for transfers between devices  47.5 us (55%)
  starting transfers between devices  17.9 us (21%)
  blocking collectives  12.1 us (14%)
  Pallas kernels  5.03 us (6%)
  local copies, waits for them, and re-layouts  1.74 us (2%)
    all_to_all x1, waiting for transfers between devices, shards(): lax.all_to_all(amplitudes.reshape(rows, depth, LANES), 'vv', split_axis=0...  47.5 us
    all_to_all x1, starting transfers between devices, shards(): lax.all_to_all(amplitudes.reshape(rows, depth, LANES), 'vv', split_axis=0...  17.9 us
    all_to_all x1, blocking collectives, shards(): lax.all_to_all(terms.reshape(slots, window, rows), 'vv', split_axis=0, co...  12.1 us
    pallas_call x1, Pallas kernels, shards(): pl.pallas_call(contract, out_shape=jax.ShapeDtypeStruct((slots * window,...  3.04 us
    pallas_call x1, Pallas kernels, shards(): pl.pallas_call(split_blocks, out_shape=[jax.ShapeDtypeStruct((slots * win...  1.99 us
    unnamed x6, local copies, waits for them, and re-layouts  1.74 us
  transfers between devices with their start and end apart: 1, of which 1 were waited for; matrix products, arithmetic and copies ran while one was open for 0% of the time, Pallas kernels for 2%

profile of v2, /device:TPU:6, one launch (start us, length us, event | category | flops | bytes accessed | tf_op | source)
XLA Modules:
  0.0 85.6 jit_solution(3472041797902534037)
XLA Ops:
  0.0 0.0 copy-start.1
  0.0 0.0 copy-start.2
  0.0 17.9 %all-to-all-start = ((f32[128,32,128]{2,1,0:T(8,128)}), f32[128,32,128]{2,1,0:T(8,128)S(1)}, u32[]{:S(2)}, u32[]{:S(2)}) async-start(f32[128,32,128]{2,1,0:T(8,128)} %bitcast.9), calls=%async_computation | async-start | bytes 4194304 | tf_op jit(solution)/shard_map/all_to_all | solution.py:62
  18.6 0.0 copy-done.1
  18.6 0.0 copy-done.2
  18.6 0.0 copy-start
  18.6 1.7 %copy-done = f32[1,4,40,4096]{3,2,1,0:T(8,128)S(1)} copy-done((f32[1,4,40,4096]{3,2,1,0:T(8,128)S(1)}, f32[1,4,40,4096]{3,2,1,0:T(8,128)}, u32[]{:S(2)}) %copy-start) | copy-done | bytes 2621464
  20.4 2.0 %split_blocks.1 = (bf16[160,4096]{1,0:T(8,128)(2,1)S(1)}, bf16[160,4096]{1,0:T(8,128)(2,1)}) custom-call(s32[16]{0:T(128)S(1)} %copy-done.1, s32[1,2]{1,0:T(1,128)S(1)} %copy-done.2, s32[1]{0:T(128)S(6)} %copy.6.count_ref, s32[1]{0:T(128)} %bitcast.member_ref, f32[4,40,4096]{2,1,0:T(8,128)S(1)} %bitcast.7), custom_call_target="tpu_custom_call" | custom-call | flops 5242880 | bytes 5242880 | tf_op jit(solution)/shard_map/split_blocks/pallas_call | solution.py:67
  22.4 47.5 %all-to-all-done = f32[128,32,128]{2,1,0:T(8,128)S(1)} async-done(((f32[128,32,128]{2,1,0:T(8,128)}), f32[128,32,128]{2,1,0:T(8,128)S(1)}, u32[]{:S(2)}, u32[]{:S(2)}) %all-to-all-start) | async-done | bytes 2097184 | tf_op jit(solution)/shard_map/all_to_all | solution.py:62
  69.9 3.0 %contract.1 = f32[160,128]{1,0:T(8,128)S(1)} custom-call(bf16[160,4096]{1,0:T(8,128)(2,1)S(1)} %get-tuple-element.7.head_ref, bf16[160,4096]{1,0:T(8,128)(2,1)} %get-tuple-element.8.tail_hbm, f32[4096,128]{1,0:T(8,128)S(1)} %bitcast.6), custom_call_target="tpu_custom_call" | custom-call | flops 671088640 | bytes 3145728 | tf_op jit(solution)/shard_map/contract/pallas_call | solution.py:82
  72.9 12.1 %all_to_all.10 = f32[4,40,128]{2,1,0:T(8,128)S(1)} all-to-all(f32[4,40,128]{2,1,0:T(8,128)S(1)} %bitcast.8), channel_id=1, replica_groups={{0,128,256,384},{4,132,260,388},{8,136,264,392},{12,140,268,396},{16,14..., dimensions={0} | all-to-all | bytes 163840 | tf_op jit(solution)/shard_map/all_to_all | solution.py:104
  85.0 0.6 fusion
Async XLA Ops:
  0.0 18.6 %copy-start.1 = (s32[16]{0:T(128)S(1)}, s32[16]{0:T(128)}, u32[]{:S(2)}) copy-start(s32[16]{0:T(128)} %tile_len_ref.1) | copy-start | bytes 196
  0.0 18.6 %copy-start.2 = (s32[1,2]{1,0:T(1,128)S(1)}, s32[1,2]{1,0:T(1,128)}, u32[]{:S(2)}) copy-start(s32[1,2]{1,0:T(1,128)} %pair_ref.1) | copy-start | bytes 28
  0.0 69.9 %all-to-all-start = ((f32[128,32,128]{2,1,0:T(8,128)}), f32[128,32,128]{2,1,0:T(8,128)S(1)}, u32[]{:S(2)}, u32[]{:S(2)}) async-start(f32[128,32,128]{2,1,0:T(8,128)} %bitcast.9), calls=%async_computation | async-start | bytes 4194304 | tf_op jit(solution)/shard_map/all_to_all | solution.py:62
  18.6 1.7 %copy-start = (f32[1,4,40,4096]{3,2,1,0:T(8,128)S(1)}, f32[1,4,40,4096]{3,2,1,0:T(8,128)}, u32[]{:S(2)}) copy-start(f32[1,4,40,4096]{3,2,1,0:T(8,128)} %param.8) | copy-start | bytes 7864324

commit v3 on v2

--- a/solution.py
+++ b/solution.py
@@ -7,6 +7,7 @@
 
 TV = 64
 LANES = 128
+CHUNKS = 2
 
 
 def split_blocks(tile_len_ref, pair_ref, count_ref, member_ref, v_ref, head_ref, tail_ref):
@@ -35,22 +36,27 @@
     return lax.dot_general(a, b, (((1,), (1,)), ((), ())), preferred_element_type=jnp.float32)
 
 
-def contract(head_ref, tail_hbm, amp_ref, out_ref, tail_ref, split_ref, sem):
+def contract(head_ref, tail_hbm, amp_ref, out_ref, tail_ref, sem):
     copy = pltpu.make_async_copy(tail_hbm, tail_ref, sem)
     copy.start()
-    rows = out_ref.shape[1]
+    half, rows = out_ref.shape
     depth = amp_ref.shape[0] // rows
-    for j in range(depth):
-        part = amp_ref[pl.ds(j, rows, stride=depth), :]
-        head = part.astype(jnp.bfloat16)
-        tail = (part - head.astype(jnp.float32)).astype(jnp.bfloat16)
-        lanes = pl.ds(j * LANES, LANES)
-        split_ref[0:rows, lanes] = head
-        split_ref[rows : 2 * rows, lanes] = tail
-    upper = times_transposed(head_ref[...], split_ref[...])
-    copy.wait()
-    lower = times_transposed(tail_ref[...], split_ref[...])
-    out_ref[...] = (lower[:, rows:] + lower[:, :rows] + upper[:, rows:]) + upper[:, :rows]
+    chunk = depth // CHUNKS
+    both = None
+    for start in range(0, depth, chunk):
+        heads, tails = [], []
+        for j in range(start, start + chunk):
+            part = amp_ref[pl.ds(j, rows, stride=depth), :]
+            heads.append(part.astype(jnp.bfloat16))
+            tails.append((part - heads[-1].astype(jnp.float32)).astype(jnp.bfloat16))
+        amp = jnp.concatenate([jnp.concatenate(heads, axis=1), jnp.concatenate(tails, axis=1)], axis=0)
+        if start == 0:
+            copy.wait()
+        lanes = pl.ds(start * LANES, chunk * LANES)
+        blocks = jnp.concatenate([head_ref[:, lanes], tail_ref[:, lanes]], axis=0)
+        product = times_transposed(blocks, amp)
+        both = product if both is None else both + product
+    out_ref[...] = (both[half:, rows:] + both[half:, :rows] + both[:half, rows:]) + both[:half, :rows]
 
 
 def shards(amplitudes, tile_len, pair_tiles, v_blocks, block_count):
@@ -90,7 +96,6 @@
         out_specs=pl.BlockSpec(memory_space=pltpu.VMEM),
         scratch_shapes=[
             pltpu.VMEM((slots * window, width), jnp.bfloat16),
-            pltpu.VMEM((2 * rows, width), jnp.bfloat16),
             pltpu.SemaphoreType.DMA,
         ],
         compiler_params=pltpu.CompilerParams(vmem_limit_bytes=16 * 1024 * 1024),

time: 85.9 us -> 85.4 us (level)
  no operation moved by 1% of the time
where the time goes in v3:
time: 85.4 us; the launch traced here: 85 us
  waiting for transfers between devices  47.5 us (56%)
  starting transfers between devices  17.9 us (21%)
  blocking collectives  12.1 us (14%)
  Pallas kernels  4.46 us (5%)
  local copies, waits for them, and re-layouts  1.74 us (2%)
    all_to_all x1, waiting for transfers between devices, shards(): lax.all_to_all(amplitudes.reshape(rows, depth, LANES), 'vv', split_axis=0...  47.5 us
    all_to_all x1, starting transfers between devices, shards(): lax.all_to_all(amplitudes.reshape(rows, depth, LANES), 'vv', split_axis=0...  17.9 us
    all_to_all x1, blocking collectives, shards(): lax.all_to_all(terms.reshape(slots, window, rows), 'vv', split_axis=0, co...  12.1 us
    pallas_call x1, Pallas kernels, shards(): pl.pallas_call(contract, out_shape=jax.ShapeDtypeStruct((slots * window,...  2.47 us
    pallas_call x1, Pallas kernels, shards(): pl.pallas_call(split_blocks, out_shape=[jax.ShapeDtypeStruct((slots * win...  1.99 us
    unnamed x6, local copies, waits for them, and re-layouts  1.74 us
  transfers between devices with their start and end apart: 1, of which 1 were waited for; matrix products, arithmetic and copies ran while one was open for 0% of the time, Pallas kernels for 2%

profile of v3, /device:TPU:6, one launch (start us, length us, event | category | flops | bytes accessed | tf_op | source)
XLA Modules:
  0.0 85.0 jit_solution(5439301481627668240)
XLA Ops:
  0.0 0.0 copy-start.1
  0.0 0.0 copy-start.2
  0.0 17.9 %all-to-all-start = ((f32[128,32,128]{2,1,0:T(8,128)}), f32[128,32,128]{2,1,0:T(8,128)S(1)}, u32[]{:S(2)}, u32[]{:S(2)}) async-start(f32[128,32,128]{2,1,0:T(8,128)} %bitcast.9), calls=%async_computation | async-start | bytes 4194304 | tf_op jit(solution)/shard_map/all_to_all | solution.py:68
  18.6 0.0 copy-done.1
  18.6 0.0 copy-done.2
  18.6 0.0 copy-start
  18.6 1.7 %copy-done = f32[1,4,40,4096]{3,2,1,0:T(8,128)S(1)} copy-done((f32[1,4,40,4096]{3,2,1,0:T(8,128)S(1)}, f32[1,4,40,4096]{3,2,1,0:T(8,128)}, u32[]{:S(2)}) %copy-start) | copy-done | bytes 2621464
  20.4 2.0 %split_blocks.1 = (bf16[160,4096]{1,0:T(8,128)(2,1)S(1)}, bf16[160,4096]{1,0:T(8,128)(2,1)}) custom-call(s32[16]{0:T(128)S(1)} %copy-done.1, s32[1,2]{1,0:T(1,128)S(1)} %copy-done.2, s32[1]{0:T(128)S(6)} %copy.6.count_ref, s32[1]{0:T(128)} %bitcast.member_ref, f32[4,40,4096]{2,1,0:T(8,128)S(1)} %bitcast.7), custom_call_target="tpu_custom_call" | custom-call | flops 5242880 | bytes 5242880 | tf_op jit(solution)/shard_map/split_blocks/pallas_call | solution.py:73
  22.4 47.5 %all-to-all-done = f32[128,32,128]{2,1,0:T(8,128)S(1)} async-done(((f32[128,32,128]{2,1,0:T(8,128)}), f32[128,32,128]{2,1,0:T(8,128)S(1)}, u32[]{:S(2)}, u32[]{:S(2)}) %all-to-all-start) | async-done | bytes 2097184 | tf_op jit(solution)/shard_map/all_to_all | solution.py:68
  69.9 2.5 %contract.1 = f32[160,128]{1,0:T(8,128)S(1)} custom-call(bf16[160,4096]{1,0:T(8,128)(2,1)S(1)} %get-tuple-element.7.head_ref, bf16[160,4096]{1,0:T(8,128)(2,1)} %get-tuple-element.8.tail_hbm, f32[4096,128]{1,0:T(8,128)S(1)} %bitcast.6), custom_call_target="tpu_custom_call" | custom-call | flops 671088640 | bytes 3145728 | tf_op jit(solution)/shard_map/contract/pallas_call | solution.py:88
  72.3 12.1 %all_to_all.10 = f32[4,40,128]{2,1,0:T(8,128)S(1)} all-to-all(f32[4,40,128]{2,1,0:T(8,128)S(1)} %bitcast.8), channel_id=1, replica_groups={{0,128,256,384},{4,132,260,388},{8,136,264,392},{12,140,268,396},{16,14..., dimensions={0} | all-to-all | bytes 163840 | tf_op jit(solution)/shard_map/all_to_all | solution.py:109
  84.4 0.6 fusion
Async XLA Ops:
  0.0 18.6 %copy-start.1 = (s32[16]{0:T(128)S(1)}, s32[16]{0:T(128)}, u32[]{:S(2)}) copy-start(s32[16]{0:T(128)} %tile_len_ref.1) | copy-start | bytes 196
  0.0 18.6 %copy-start.2 = (s32[1,2]{1,0:T(1,128)S(1)}, s32[1,2]{1,0:T(1,128)}, u32[]{:S(2)}) copy-start(s32[1,2]{1,0:T(1,128)} %pair_ref.1) | copy-start | bytes 28
  0.0 69.9 %all-to-all-start = ((f32[128,32,128]{2,1,0:T(8,128)}), f32[128,32,128]{2,1,0:T(8,128)S(1)}, u32[]{:S(2)}, u32[]{:S(2)}) async-start(f32[128,32,128]{2,1,0:T(8,128)} %bitcast.9), calls=%async_computation | async-start | bytes 4194304 | tf_op jit(solution)/shard_map/all_to_all | solution.py:68
  18.6 1.7 %copy-start = (f32[1,4,40,4096]{3,2,1,0:T(8,128)S(1)}, f32[1,4,40,4096]{3,2,1,0:T(8,128)}, u32[]{:S(2)}) copy-start(f32[1,4,40,4096]{3,2,1,0:T(8,128)} %param.8) | copy-start | bytes 7864324

commit v4 on v3

--- a/solution.py
+++ b/solution.py
@@ -10,20 +10,18 @@
 CHUNKS = 2
 
 
-def split_blocks(tile_len_ref, pair_ref, count_ref, member_ref, v_ref, head_ref, tail_ref):
+def split_blocks(tile_len_ref, pair_ref, count_ref, v_ref, head_ref, tail_ref):
     slots, window, width = v_ref.shape
     c_length = tile_len_ref[pair_ref[0, 0]]
     d_length = tile_len_ref[pair_ref[0, 1]]
     count = count_ref[0]
-    member = member_ref[0]
     step = 4 * LANES
     for start in range(0, width, step):
         lanes = pl.ds(start, step)
         index = lax.broadcasted_iota(jnp.int32, (window, step), 1) + start
         inside = (index // TV < c_length) & (index % TV < d_length)
         blocks = []
-        for target in range(slots):
-            slot = lax.rem(target - member + slots, slots)
+        for slot in range(slots):
             live = jnp.where(slot < count, 1, 0)
             blocks.append(jnp.where(inside & (live > 0), v_ref[slot, :, lanes], 0.0))
         block = jnp.concatenate(blocks, axis=0)
@@ -36,10 +34,12 @@
     return lax.dot_general(a, b, (((1,), (1,)), ((), ())), preferred_element_type=jnp.float32)
 
 
-def contract(head_ref, tail_hbm, amp_ref, out_ref, tail_ref, sem):
+def contract(head_ref, tail_hbm, amp_ref, *refs):
+    *out_refs, tail_ref, sem = refs
     copy = pltpu.make_async_copy(tail_hbm, tail_ref, sem)
     copy.start()
-    half, rows = out_ref.shape
+    window, rows = out_refs[0].shape
+    half = window * len(out_refs)
     depth = amp_ref.shape[0] // rows
     chunk = depth // CHUNKS
     both = None
@@ -56,7 +56,9 @@
         blocks = jnp.concatenate([head_ref[:, lanes], tail_ref[:, lanes]], axis=0)
         product = times_transposed(blocks, amp)
         both = product if both is None else both + product
-    out_ref[...] = (both[half:, rows:] + both[half:, :rows] + both[:half, rows:]) + both[:half, :rows]
+    total = (both[half:, rows:] + both[half:, :rows] + both[:half, rows:]) + both[:half, :rows]
+    for slot, out_ref in enumerate(out_refs):
+        out_ref[...] = total[slot * window : (slot + 1) * window]
 
 
 def shards(amplitudes, tile_len, pair_tiles, v_blocks, block_count):
@@ -69,31 +71,30 @@
         amplitudes.reshape(rows, depth, LANES), "vv", split_axis=0, concat_axis=0, tiled=True
     )
 
-    member = lax.axis_index("vv") // stride
     heads, tails = pl.pallas_call(
         split_blocks,
         out_shape=[
             jax.ShapeDtypeStruct((slots * window, width), jnp.bfloat16),
             pltpu.HBM((slots * window, width), jnp.bfloat16),
         ],
-        in_specs=[pl.BlockSpec(memory_space=pltpu.SMEM)] * 4 + [pl.BlockSpec(memory_space=pltpu.VMEM)],
+        in_specs=[pl.BlockSpec(memory_space=pltpu.SMEM)] * 3 + [pl.BlockSpec(memory_space=pltpu.VMEM)],
         out_specs=[pl.BlockSpec(memory_space=pltpu.VMEM)] * 2,
         compiler_params=pltpu.CompilerParams(vmem_limit_bytes=16 * 1024 * 1024),
         cost_estimate=pl.CostEstimate(
             flops=8 * slots * window * width, bytes_accessed=8 * slots * window * width, transcendentals=0
         ),
         name="split_blocks",
-    )(tile_len, pair_tiles, block_count, member.astype(jnp.int32)[None], v_blocks[0])
+    )(tile_len, pair_tiles, block_count, v_blocks[0])
 
     terms = pl.pallas_call(
         contract,
-        out_shape=jax.ShapeDtypeStruct((slots * window, rows), jnp.float32),
+        out_shape=[jax.ShapeDtypeStruct((window, rows), jnp.float32)] * slots,
         in_specs=[
             pl.BlockSpec(memory_space=pltpu.VMEM),
             pl.BlockSpec(memory_space=pl.ANY),
             pl.BlockSpec(memory_space=pltpu.VMEM),
         ],
-        out_specs=pl.BlockSpec(memory_space=pltpu.VMEM),
+        out_specs=[pl.BlockSpec(memory_space=pltpu.VMEM)] * slots,
         scratch_shapes=[
             pltpu.VMEM((slots * window, width), jnp.bfloat16),
             pltpu.SemaphoreType.DMA,
@@ -105,11 +106,13 @@
         name="contract",
     )(heads, pltpu.with_memory_space_constraint(tails, pltpu.HBM), arrived.reshape(rows * depth, LANES))
 
-    groups = [[i + stride * k for k in range(slots)] for i in range(stride)]
-    moved = lax.all_to_all(
-        terms.reshape(slots, window, rows), "vv", split_axis=0, concat_axis=0, axis_index_groups=groups, tiled=True
-    )
-    total = (moved[0] + moved[1]) + (moved[2] + moved[3])
+    moved = {}
+    for slot in sorted(range(1, slots), key=lambda k: abs(k - slots // 2)):
+        route = [(i, (i + slot * stride) % owners) for i in range(owners)]
+        moved[slot] = lax.ppermute(terms[slot], "vv", route)
+    total = terms[0]
+    for slot in range(1, slots):
+        total = total + moved[slot]
     return total.reshape(1, window, 1, rows)
 
 

time: 85.4 us -> 88.9 us (1.041)
  blocking collectives: 12.1 us -> 0 us
  starting transfers between devices: 17.9 us -> 29.9 us
  waiting for transfers between devices: 47.5 us -> 50.3 us
    all_to_all x1 -> x0, blocking collectives: 12.1 us -> none  [shards(): lax.all_to_all(terms.reshape(slots, window, rows), 'vv', split_axis=0, co...]
    ppermute x0 -> x3, starting transfers between devices: none -> 12 us  [shards(): moved[slot] = lax.ppermute(terms[slot], 'vv', route)]
    ppermute x0 -> x3, waiting for transfers between devices: none -> 2.75 us  [shards(): moved[slot] = lax.ppermute(terms[slot], 'vv', route)]
  transfers between devices with their start and end apart: 1 -> 4, of which waited for: 1 -> 3; matrix products, arithmetic and copies ran while one was open for 0% -> 0% of each run, Pallas kernels for 2% -> 2%
where the time goes in v4:
time: 88.9 us; the launch traced here: 87.7 us
  waiting for transfers between devices  50.3 us (57%)
  starting transfers between devices  29.9 us (34%)
  Pallas kernels  4.45 us (5%)
  local copies, waits for them, and re-layouts  1.74 us (2%)
    all_to_all x1, waiting for transfers between devices, shards(): lax.all_to_all(amplitudes.reshape(rows, depth, LANES), 'vv', split_axis=0...  47.5 us
    all_to_all x1, starting transfers between devices, shards(): lax.all_to_all(amplitudes.reshape(rows, depth, LANES), 'vv', split_axis=0...  17.9 us
    ppermute x3, starting transfers between devices, shards(): moved[slot] = lax.ppermute(terms[slot], 'vv', route)  12 us
    ppermute x3, waiting for transfers between devices, shards(): moved[slot] = lax.ppermute(terms[slot], 'vv', route)  2.75 us
    pallas_call x1, Pallas kernels, shards(): pl.pallas_call(contract, out_shape=[jax.ShapeDtypeStruct((window, rows),...  2.44 us
    pallas_call x1, Pallas kernels, shards(): pl.pallas_call(split_blocks, out_shape=[jax.ShapeDtypeStruct((slots * win...  2 us
  transfers between devices with their start and end apart: 4, of which 3 were waited for; matrix products, arithmetic and copies ran while one was open for 0% of the time, Pallas kernels for 2%

profile of v4, /device:TPU:6, one launch (start us, length us, event | category | flops | bytes accessed | tf_op | source)
XLA Modules:
  0.0 87.7 jit_solution(546240835044194450)
XLA Ops:
  0.0 0.0 copy-start.1
  0.0 0.0 copy-start.2
  0.0 17.9 %all-to-all-start = ((f32[128,32,128]{2,1,0:T(8,128)}), f32[128,32,128]{2,1,0:T(8,128)S(1)}, u32[]{:S(2)}, u32[]{:S(2)}) async-start(f32[128,32,128]{2,1,0:T(8,128)} %bitcast.8), calls=%async_computation | async-start | bytes 4194304 | tf_op jit(solution)/shard_map/all_to_all | solution.py:70
  18.6 0.0 copy-done.1
  18.6 0.0 copy-done.2
  18.6 0.0 copy-start
  18.6 1.7 %copy-done = f32[1,4,40,4096]{3,2,1,0:T(8,128)S(1)} copy-done((f32[1,4,40,4096]{3,2,1,0:T(8,128)S(1)}, f32[1,4,40,4096]{3,2,1,0:T(8,128)}, u32[]{:S(2)}) %copy-start) | copy-done | bytes 2621464
  20.4 2.0 %split_blocks.1 = (bf16[160,4096]{1,0:T(8,128)(2,1)S(1)}, bf16[160,4096]{1,0:T(8,128)(2,1)}) custom-call(s32[16]{0:T(128)S(1)} %copy-done.1, s32[1,2]{1,0:T(1,128)S(1)} %copy-done.2, s32[1]{0:T(128)S(6)} %copy.7.count_ref, f32[4,40,4096]{2,1,0:T(8,128)S(1)} %bitcast.7), custom_call_target="tpu_custom_call" | custom-call | flops 5242880 | bytes 5242880 | tf_op jit(solution)/shard_map/split_blocks/pallas_call | solution.py:74
  22.4 47.5 %all-to-all-done = f32[128,32,128]{2,1,0:T(8,128)S(1)} async-done(((f32[128,32,128]{2,1,0:T(8,128)}), f32[128,32,128]{2,1,0:T(8,128)S(1)}, u32[]{:S(2)}, u32[]{:S(2)}) %all-to-all-start) | async-done | bytes 2097184 | tf_op jit(solution)/shard_map/all_to_all | solution.py:70
  69.9 2.4 %contract.1 = (f32[40,128]{1,0:T(8,128)S(1)}, f32[40,128]{1,0:T(8,128)S(1)}, f32[40,128]{1,0:T(8,128)S(1)}, f32[40,128]{1,0:T(8,128)S(1)}) custom-call(bf16[160,4096]{1,0:T(8,128)(2,1)S(1)} %get-tuple-element.11.head_ref, bf16[160,4096]{1,0:T(8,128)(2,1)} %get-tuple-element.12.tail_hbm, f32[4096,128]{1,0:T(8,128)S(1)} %bitcast.6), custom_call_target="tpu_custom_call" | custom-call | flops 671088640 | bytes 3145728 | tf_op jit(solution)/shard_map/contract/pallas_call | solution.py:89
  72.3 2.9 %collective-permute-start = (f32[40,128]{1,0:T(8,128)S(1)}, f32[40,128]{1,0:T(8,128)S(1)}, u32[]{:S(2)}, u32[]{:S(2)}) collective-permute-start(f32[40,128]{1,0:T(8,128)S(1)} %get-tuple-element.14), channel_id=1, source_target_pairs={{0,128},{4,132},{8,136},{12,140},{16,144},{20,148},{24,152},{28,15... | collective-permute-start | bytes 61448 | tf_op jit(solution)/shard_map/ppermute | solution.py:112
  75.2 5.2 %collective-permute-start.1 = (f32[40,128]{1,0:T(8,128)S(1)}, f32[40,128]{1,0:T(8,128)S(1)}, u32[]{:S(2)}, u32[]{:S(2)}) collective-permute-start(f32[40,128]{1,0:T(8,128)S(1)} %get-tuple-element.15), channel_id=1, source_target_pairs={{0,256},{4,260},{8,264},{12,268},{16,272},{20,276},{24,280},{28,28... | collective-permute-start | bytes 61448 | tf_op jit(solution)/shard_map/ppermute | solution.py:112
  80.4 3.9 %collective-permute-start.2 = (f32[40,128]{1,0:T(8,128)S(1)}, f32[40,128]{1,0:T(8,128)S(1)}, u32[]{:S(2)}, u32[]{:S(2)}) collective-permute-start(f32[40,128]{1,0:T(8,128)S(1)} %get-tuple-element.16), channel_id=1, source_target_pairs={{0,384},{4,388},{8,392},{12,396},{16,400},{20,404},{24,408},{28,41... | collective-permute-start | bytes 61448 | tf_op jit(solution)/shard_map/ppermute | solution.py:112
  84.3 0.0 collective-permute-done
  84.3 0.5 collective-permute-done.1
  84.8 2.3 %collective-permute-done.2 = f32[40,128]{1,0:T(8,128)S(1)} collective-permute-done((f32[40,128]{1,0:T(8,128)S(1)}, f32[40,128]{1,0:T(8,128)S(1)}, u32[]{:S(2)}, u32[]{:S(2)}) %collective-permute-start.2) | collective-permute-done | bytes 20512 | tf_op jit(solution)/shard_map/ppermute | solution.py:112
  87.1 0.6 add_add_fusion
Async XLA Ops:
  0.0 18.6 %copy-start.1 = (s32[16]{0:T(128)S(1)}, s32[16]{0:T(128)}, u32[]{:S(2)}) copy-start(s32[16]{0:T(128)} %tile_len_ref.1) | copy-start | bytes 196
  0.0 18.6 %copy-start.2 = (s32[1,2]{1,0:T(1,128)S(1)}, s32[1,2]{1,0:T(1,128)}, u32[]{:S(2)}) copy-start(s32[1,2]{1,0:T(1,128)} %pair_ref.1) | copy-start | bytes 28
  0.0 69.9 %all-to-all-start = ((f32[128,32,128]{2,1,0:T(8,128)}), f32[128,32,128]{2,1,0:T(8,128)S(1)}, u32[]{:S(2)}, u32[]{:S(2)}) async-start(f32[128,32,128]{2,1,0:T(8,128)} %bitcast.8), calls=%async_computation | async-start | bytes 4194304 | tf_op jit(solution)/shard_map/all_to_all | solution.py:70
  18.6 1.7 %copy-start = (f32[1,4,40,4096]{3,2,1,0:T(8,128)S(1)}, f32[1,4,40,4096]{3,2,1,0:T(8,128)}, u32[]{:S(2)}) copy-start(f32[1,4,40,4096]{3,2,1,0:T(8,128)} %param.8) | copy-start | bytes 7864324
  72.3 12.0 %collective-permute-start = (f32[40,128]{1,0:T(8,128)S(1)}, f32[40,128]{1,0:T(8,128)S(1)}, u32[]{:S(2)}, u32[]{:S(2)}) collective-permute-start(f32[40,128]{1,0:T(8,128)S(1)} %get-tuple-element.14), channel_id=1, source_target_pairs={{0,128},{4,132},{8,136},{12,140},{16,144},{20,148},{24,152},{28,15... | collective-permute-start | bytes 61448 | tf_op jit(solution)/shard_map/ppermute | solution.py:112
  75.2 9.6 %collective-permute-start.1 = (f32[40,128]{1,0:T(8,128)S(1)}, f32[40,128]{1,0:T(8,128)S(1)}, u32[]{:S(2)}, u32[]{:S(2)}) collective-permute-start(f32[40,128]{1,0:T(8,128)S(1)} %get-tuple-element.15), channel_id=1, source_target_pairs={{0,256},{4,260},{8,264},{12,268},{16,272},{20,276},{24,280},{28,28... | collective-permute-start | bytes 61448 | tf_op jit(solution)/shard_map/ppermute | solution.py:112
  80.4 6.7 %collective-permute-start.2 = (f32[40,128]{1,0:T(8,128)S(1)}, f32[40,128]{1,0:T(8,128)S(1)}, u32[]{:S(2)}, u32[]{:S(2)}) collective-permute-start(f32[40,128]{1,0:T(8,128)S(1)} %get-tuple-element.16), channel_id=1, source_target_pairs={{0,384},{4,388},{8,392},{12,396},{16,400},{20,404},{24,408},{28,41... | collective-permute-start | bytes 61448 | tf_op jit(solution)/shard_map/ppermute | solution.py:112

commit v5 on v3

--- a/solution.py
+++ b/solution.py
@@ -10,7 +10,7 @@
 CHUNKS = 2
 
 
-def split_blocks(tile_len_ref, pair_ref, count_ref, member_ref, v_ref, head_ref, tail_ref):
+def split_blocks(tile_len_ref, pair_ref, count_ref, member_ref, v_ref, head_ref, tail_ref, own_ref):
     slots, window, width = v_ref.shape
     c_length = tile_len_ref[pair_ref[0, 0]]
     d_length = tile_len_ref[pair_ref[0, 1]]
@@ -24,12 +24,15 @@
         blocks = []
         for target in range(slots):
             slot = lax.rem(target - member + slots, slots)
-            live = jnp.where(slot < count, 1, 0)
+            live = jnp.where((slot < count) & (slot > 0), 1, 0)
             blocks.append(jnp.where(inside & (live > 0), v_ref[slot, :, lanes], 0.0))
         block = jnp.concatenate(blocks, axis=0)
         head = block.astype(jnp.bfloat16)
         head_ref[:, lanes] = head
         tail_ref[:, lanes] = (block - head.astype(jnp.float32)).astype(jnp.bfloat16)
+        own = jnp.where(inside & (count > 0), v_ref[0, :, lanes], 0.0)
+        above = own.astype(jnp.bfloat16).astype(jnp.float32)
+        own_ref[:, lanes] = jnp.concatenate([above, own - above], axis=0).astype(jnp.bfloat16)
 
 
 def times_transposed(a, b):
@@ -59,6 +62,23 @@
     out_ref[...] = (both[half:, rows:] + both[half:, :rows] + both[:half, rows:]) + both[:half, :rows]
 
 
+def contract_own(own_ref, amp_ref, out_ref):
+    window, rows = out_ref.shape
+    depth = amp_ref.shape[0] // rows
+    chunk = depth // CHUNKS
+    both = None
+    for start in range(0, depth, chunk):
+        heads, tails = [], []
+        for j in range(start, start + chunk):
+            part = amp_ref[pl.ds(j, rows, stride=depth), :]
+            heads.append(part.astype(jnp.bfloat16))
+            tails.append((part - heads[-1].astype(jnp.float32)).astype(jnp.bfloat16))
+        amp = jnp.concatenate([jnp.concatenate(heads, axis=1), jnp.concatenate(tails, axis=1)], axis=0)
+        product = times_transposed(own_ref[:, pl.ds(start * LANES, chunk * LANES)], amp)
+        both = product if both is None else both + product
+    out_ref[...] = (both[window:, rows:] + both[window:, :rows] + both[:window, rows:]) + both[:window, :rows]
+
+
 def shards(amplitudes, tile_len, pair_tiles, v_blocks, block_count):
     owners = lax.axis_size("vv")
     slots, window, width = v_blocks.shape[1:]
@@ -70,14 +90,15 @@
     )
 
     member = lax.axis_index("vv") // stride
-    heads, tails = pl.pallas_call(
+    heads, tails, own = pl.pallas_call(
         split_blocks,
         out_shape=[
             jax.ShapeDtypeStruct((slots * window, width), jnp.bfloat16),
             pltpu.HBM((slots * window, width), jnp.bfloat16),
+            pltpu.HBM((2 * window, width), jnp.bfloat16),
         ],
         in_specs=[pl.BlockSpec(memory_space=pltpu.SMEM)] * 4 + [pl.BlockSpec(memory_space=pltpu.VMEM)],
-        out_specs=[pl.BlockSpec(memory_space=pltpu.VMEM)] * 2,
+        out_specs=[pl.BlockSpec(memory_space=pltpu.VMEM)] * 3,
         compiler_params=pltpu.CompilerParams(vmem_limit_bytes=16 * 1024 * 1024),
         cost_estimate=pl.CostEstimate(
             flops=8 * slots * window * width, bytes_accessed=8 * slots * window * width, transcendentals=0
@@ -105,11 +126,23 @@
         name="contract",
     )(heads, pltpu.with_memory_space_constraint(tails, pltpu.HBM), arrived.reshape(rows * depth, LANES))
 
+    mine = pl.pallas_call(
+        contract_own,
+        out_shape=jax.ShapeDtypeStruct((window, rows), jnp.float32),
+        in_specs=[pl.BlockSpec(memory_space=pltpu.VMEM)] * 2,
+        out_specs=pl.BlockSpec(memory_space=pltpu.VMEM),
+        compiler_params=pltpu.CompilerParams(vmem_limit_bytes=16 * 1024 * 1024),
+        cost_estimate=pl.CostEstimate(
+            flops=8 * slots * window * rows * width, bytes_accessed=6 * rows * width, transcendentals=0
+        ),
+        name="contract_own",
+    )(own, arrived.reshape(rows * depth, LANES))
+
     groups = [[i + stride * k for k in range(slots)] for i in range(stride)]
     moved = lax.all_to_all(
         terms.reshape(slots, window, rows), "vv", split_axis=0, concat_axis=0, axis_index_groups=groups, tiled=True
     )
-    total = (moved[0] + moved[1]) + (moved[2] + moved[3])
+    total = ((moved[0] + moved[1]) + (moved[2] + moved[3])) + mine
     return total.reshape(1, window, 1, rows)
 
 

time: 85.4 us -> 86.3 us (1.011)
  blocking collectives: 12.1 us -> 0 us
  waiting for transfers between devices: 47.5 us -> 53.5 us
  starting transfers between devices: 17.9 us -> 21.3 us
  Pallas kernels: 4.46 us -> 6.87 us
  local copies, waits for them, and re-layouts: 1.74 us -> 2.83 us
    all_to_all x1 -> x0, blocking collectives: 12.1 us -> none  [shards(): lax.all_to_all(terms.reshape(slots, window, rows), 'vv', split_axis=0, co...]
    all_to_all x0 -> x1, waiting for transfers between devices: none -> 6.37 us  [shards(): lax.all_to_all(terms.reshape(slots, window, rows), 'vv', split_axis=0, co...]
    all_to_all x0 -> x1, starting transfers between devices: none -> 3.37 us  [shards(): lax.all_to_all(terms.reshape(slots, window, rows), 'vv', split_axis=0, co...]
    pallas_call x0 -> x1, Pallas kernels: none -> 1.46 us  [shards(): pl.pallas_call(contract_own, out_shape=jax.ShapeDtypeStruct((window, rows...]
    unnamed x6 -> x8, local copies, waits for them, and re-layouts: 1.74 us -> 2.83 us
  transfers between devices with their start and end apart: 1 -> 2, of which waited for: 1 -> 2; matrix products, arithmetic and copies ran while one was open for 0% -> 0% of each run, Pallas kernels for 2% -> 4%
where the time goes in v5:
time: 86.3 us; the launch traced here: 85.9 us
  waiting for transfers between devices  53.5 us (62%)
  starting transfers between devices  21.3 us (25%)
  Pallas kernels  6.87 us (8%)
  local copies, waits for them, and re-layouts  2.83 us (3%)
    all_to_all x1, waiting for transfers between devices, shards(): lax.all_to_all(amplitudes.reshape(rows, depth, LANES), 'vv', split_axis=0...  47.2 us
    all_to_all x1, starting transfers between devices, shards(): lax.all_to_all(amplitudes.reshape(rows, depth, LANES), 'vv', split_axis=0...  17.9 us
    all_to_all x1, waiting for transfers between devices, shards(): lax.all_to_all(terms.reshape(slots, window, rows), 'vv', split_axis=0, co...  6.37 us
    all_to_all x1, starting transfers between devices, shards(): lax.all_to_all(terms.reshape(slots, window, rows), 'vv', split_axis=0, co...  3.37 us
    pallas_call x1, Pallas kernels, shards(): pl.pallas_call(contract, out_shape=jax.ShapeDtypeStruct((slots * window,...  3.09 us
    unnamed x8, local copies, waits for them, and re-layouts  2.83 us
    pallas_call x1, Pallas kernels, shards(): pl.pallas_call(split_blocks, out_shape=[jax.ShapeDtypeStruct((slots * win...  2.32 us
  transfers between devices with their start and end apart: 2, of which 2 were waited for; matrix products, arithmetic and copies ran while one was open for 0% of the time, Pallas kernels for 4%

profile of v5, /device:TPU:6, one launch (start us, length us, event | category | flops | bytes accessed | tf_op | source)
XLA Modules:
  0.0 85.9 jit_solution(11606449915262999868)
XLA Ops:
  0.0 0.0 copy-start.2
  0.0 0.0 copy-start.3
  0.0 17.9 %all-to-all-start = ((f32[128,32,128]{2,1,0:T(8,128)}), f32[128,32,128]{2,1,0:T(8,128)S(1)}, u32[]{:S(2)}, u32[]{:S(2)}) async-start(f32[128,32,128]{2,1,0:T(8,128)} %bitcast.15), calls=%async_computation | async-start | bytes 4194304 | tf_op jit(solution)/shard_map/all_to_all | solution.py:88
  18.6 0.0 copy-done.2
  18.6 0.0 copy-done.3
  18.6 0.0 copy-start
  18.6 1.7 %copy-done = f32[1,4,40,4096]{3,2,1,0:T(8,128)S(1)} copy-done((f32[1,4,40,4096]{3,2,1,0:T(8,128)S(1)}, f32[1,4,40,4096]{3,2,1,0:T(8,128)}, u32[]{:S(2)}) %copy-start) | copy-done | bytes 2621464
  20.4 2.3 %split_blocks.1 = (bf16[160,4096]{1,0:T(8,128)(2,1)S(1)}, bf16[160,4096]{1,0:T(8,128)(2,1)}, bf16[80,4096]{1,0:T(8,128)(2,1)}) custom-call(s32[16]{0:T(128)S(1)} %copy-done.2, s32[1,2]{1,0:T(1,128)S(1)} %copy-done.3, s32[1]{0:T(128)S(6)} %copy.7.count_ref, s32[1]{0:T(128)} %bitcast.member_ref, f32[4,40,4096]{2,1,0:T(8,128)S(1)} %bitcast.14), custom_call_target="tpu_custom_call" | custom-call | flops 5242880 | bytes 5242880 | tf_op jit(solution)/shard_map/split_blocks/pallas_call | solution.py:93
  22.7 47.2 %all-to-all-done = f32[128,32,128]{2,1,0:T(8,128)S(1)} async-done(((f32[128,32,128]{2,1,0:T(8,128)}), f32[128,32,128]{2,1,0:T(8,128)S(1)}, u32[]{:S(2)}, u32[]{:S(2)}) %all-to-all-start) | async-done | bytes 2097184 | tf_op jit(solution)/shard_map/all_to_all | solution.py:88
  69.9 3.1 %contract.1 = f32[160,128]{1,0:T(8,128)} custom-call(bf16[160,4096]{1,0:T(8,128)(2,1)S(1)} %get-tuple-element.8.head_ref, bf16[160,4096]{1,0:T(8,128)(2,1)} %get-tuple-element.9.tail_hbm, f32[4096,128]{1,0:T(8,128)S(1)} %bitcast.12), custom_call_target="tpu_custom_call" | custom-call | flops 671088640 | bytes 3145728 | tf_op jit(solution)/shard_map/contract/pallas_call | solution.py:109
  73.0 3.4 %all-to-all-start.1 = ((f32[4,40,128]{2,1,0:T(8,128)}), f32[4,40,128]{2,1,0:T(8,128)S(1)}, u32[]{:S(2)}, u32[]{:S(2)}) async-start(f32[4,40,128]{2,1,0:T(8,128)} %bitcast.4), calls=%async_computation.1 | async-start | bytes 163840 | tf_op jit(solution)/shard_map/all_to_all | solution.py:142
  76.3 0.0 copy-start.1
  76.3 1.1 %copy-done.1 = bf16[80,4096]{1,0:T(8,128)(2,1)S(1)} copy-done((bf16[80,4096]{1,0:T(8,128)(2,1)S(1)}, bf16[80,4096]{1,0:T(8,128)(2,1)}, u32[]{:S(2)}) %copy-start.1) | copy-done | bytes 655384
  77.4 1.5 %contract_own.1 = f32[40,128]{1,0:T(8,128)S(1)} custom-call(bf16[80,4096]{1,0:T(8,128)(2,1)S(1)} %copy-done.1, f32[4096,128]{1,0:T(8,128)S(1)} %bitcast.13), custom_call_target="tpu_custom_call" | custom-call | flops 671088640 | bytes 3145728 | tf_op jit(solution)/shard_map/contract_own/pallas_call | solution.py:129
  78.9 6.4 %all-to-all-done.1 = f32[4,40,128]{2,1,0:T(8,128)S(1)} async-done(((f32[4,40,128]{2,1,0:T(8,128)}), f32[4,40,128]{2,1,0:T(8,128)S(1)}, u32[]{:S(2)}, u32[]{:S(2)}) %all-to-all-start.1) | async-done | bytes 81952 | tf_op jit(solution)/shard_map/all_to_all | solution.py:142
  85.3 0.6 fusion.2
Async XLA Ops:
  0.0 18.6 %copy-start.2 = (s32[16]{0:T(128)S(1)}, s32[16]{0:T(128)}, u32[]{:S(2)}) copy-start(s32[16]{0:T(128)} %tile_len_ref.1) | copy-start | bytes 196
  0.0 18.6 %copy-start.3 = (s32[1,2]{1,0:T(1,128)S(1)}, s32[1,2]{1,0:T(1,128)}, u32[]{:S(2)}) copy-start(s32[1,2]{1,0:T(1,128)} %pair_ref.1) | copy-start | bytes 28
  0.0 69.9 %all-to-all-start = ((f32[128,32,128]{2,1,0:T(8,128)}), f32[128,32,128]{2,1,0:T(8,128)S(1)}, u32[]{:S(2)}, u32[]{:S(2)}) async-start(f32[128,32,128]{2,1,0:T(8,128)} %bitcast.15), calls=%async_computation | async-start | bytes 4194304 | tf_op jit(solution)/shard_map/all_to_all | solution.py:88
  18.6 1.7 %copy-start = (f32[1,4,40,4096]{3,2,1,0:T(8,128)S(1)}, f32[1,4,40,4096]{3,2,1,0:T(8,128)}, u32[]{:S(2)}) copy-start(f32[1,4,40,4096]{3,2,1,0:T(8,128)} %param.8) | copy-start | bytes 7864324
  73.0 12.3 %all-to-all-start.1 = ((f32[4,40,128]{2,1,0:T(8,128)}), f32[4,40,128]{2,1,0:T(8,128)S(1)}, u32[]{:S(2)}, u32[]{:S(2)}) async-start(f32[4,40,128]{2,1,0:T(8,128)} %bitcast.4), calls=%async_computation.1 | async-start | bytes 163840 | tf_op jit(solution)/shard_map/all_to_all | solution.py:142
  76.3 1.1 %copy-start.1 = (bf16[80,4096]{1,0:T(8,128)(2,1)S(1)}, bf16[80,4096]{1,0:T(8,128)(2,1)}, u32[]{:S(2)}) copy-start(bf16[80,4096]{1,0:T(8,128)(2,1)} %get-tuple-element.10.own_ref) | copy-start | bytes 1966084

commit v6 on v5

--- a/solution.py
+++ b/solution.py
@@ -10,39 +10,39 @@
 CHUNKS = 2
 
 
-def split_blocks(tile_len_ref, pair_ref, count_ref, member_ref, v_ref, head_ref, tail_ref, own_ref):
+def split_blocks(tile_len_ref, pair_ref, count_ref, v_ref, head_ref, tail_ref, own_ref):
     slots, window, width = v_ref.shape
     c_length = tile_len_ref[pair_ref[0, 0]]
     d_length = tile_len_ref[pair_ref[0, 1]]
     count = count_ref[0]
-    member = member_ref[0]
     step = 4 * LANES
+    spare = head_ref.shape[0] - (slots - 1) * window
     for start in range(0, width, step):
         lanes = pl.ds(start, step)
         index = lax.broadcasted_iota(jnp.int32, (window, step), 1) + start
         inside = (index // TV < c_length) & (index % TV < d_length)
-        blocks = []
-        for target in range(slots):
-            slot = lax.rem(target - member + slots, slots)
-            live = jnp.where((slot < count) & (slot > 0), 1, 0)
-            blocks.append(jnp.where(inside & (live > 0), v_ref[slot, :, lanes], 0.0))
-        block = jnp.concatenate(blocks, axis=0)
+        kept = []
+        for slot in range(slots):
+            live = jnp.where(slot < count, 1, 0)
+            kept.append(jnp.where(inside & (live > 0), v_ref[slot, :, lanes], 0.0))
+        padding = [jnp.zeros((spare, step), jnp.float32)] if spare else []
+        block = jnp.concatenate(kept[1:] + padding, axis=0)
         head = block.astype(jnp.bfloat16)
         head_ref[:, lanes] = head
         tail_ref[:, lanes] = (block - head.astype(jnp.float32)).astype(jnp.bfloat16)
-        own = jnp.where(inside & (count > 0), v_ref[0, :, lanes], 0.0)
-        above = own.astype(jnp.bfloat16).astype(jnp.float32)
-        own_ref[:, lanes] = jnp.concatenate([above, own - above], axis=0).astype(jnp.bfloat16)
+        above = kept[0].astype(jnp.bfloat16).astype(jnp.float32)
+        own_ref[:, lanes] = jnp.concatenate([above, kept[0] - above], axis=0).astype(jnp.bfloat16)
 
 
 def times_transposed(a, b):
     return lax.dot_general(a, b, (((1,), (1,)), ((), ())), preferred_element_type=jnp.float32)
 
 
-def contract(head_ref, tail_hbm, amp_ref, out_ref, tail_ref, sem):
+def contract(member_ref, head_ref, tail_hbm, amp_ref, out_ref, tail_ref, sem):
     copy = pltpu.make_async_copy(tail_hbm, tail_ref, sem)
     copy.start()
-    half, rows = out_ref.shape
+    slots, window, rows = out_ref.shape
+    half = head_ref.shape[0]
     depth = amp_ref.shape[0] // rows
     chunk = depth // CHUNKS
     both = None
@@ -59,7 +59,11 @@
         blocks = jnp.concatenate([head_ref[:, lanes], tail_ref[:, lanes]], axis=0)
         product = times_transposed(blocks, amp)
         both = product if both is None else both + product
-    out_ref[...] = (both[half:, rows:] + both[half:, :rows] + both[:half, rows:]) + both[:half, :rows]
+    total = (both[half:, rows:] + both[half:, :rows] + both[:half, rows:]) + both[:half, :rows]
+    member = member_ref[0]
+    out_ref[member] = jnp.zeros((window, rows), jnp.float32)
+    for slot in range(1, slots):
+        out_ref[lax.rem(member + slot, slots)] = total[(slot - 1) * window : slot * window]
 
 
 def contract_own(own_ref, amp_ref, out_ref):
@@ -90,41 +94,45 @@
     )
 
     member = lax.axis_index("vv") // stride
+    remote = -(-(slots - 1) * window // 16) * 16
     heads, tails, own = pl.pallas_call(
         split_blocks,
         out_shape=[
-            jax.ShapeDtypeStruct((slots * window, width), jnp.bfloat16),
-            pltpu.HBM((slots * window, width), jnp.bfloat16),
+            jax.ShapeDtypeStruct((remote, width), jnp.bfloat16),
+            pltpu.HBM((remote, width), jnp.bfloat16),
             pltpu.HBM((2 * window, width), jnp.bfloat16),
         ],
-        in_specs=[pl.BlockSpec(memory_space=pltpu.SMEM)] * 4 + [pl.BlockSpec(memory_space=pltpu.VMEM)],
+        in_specs=[pl.BlockSpec(memory_space=pltpu.SMEM)] * 3 + [pl.BlockSpec(memory_space=pltpu.VMEM)],
         out_specs=[pl.BlockSpec(memory_space=pltpu.VMEM)] * 3,
         compiler_params=pltpu.CompilerParams(vmem_limit_bytes=16 * 1024 * 1024),
         cost_estimate=pl.CostEstimate(
             flops=8 * slots * window * width, bytes_accessed=8 * slots * window * width, transcendentals=0
         ),
         name="split_blocks",
-    )(tile_len, pair_tiles, block_count, member.astype(jnp.int32)[None], v_blocks[0])
+    )(tile_len, pair_tiles, block_count, v_blocks[0])
 
     terms = pl.pallas_call(
         contract,
-        out_shape=jax.ShapeDtypeStruct((slots * window, rows), jnp.float32),
+        out_shape=pltpu.VMEM((slots, window, rows), jnp.float32),
         in_specs=[
+            pl.BlockSpec(memory_space=pltpu.SMEM),
             pl.BlockSpec(memory_space=pltpu.VMEM),
             pl.BlockSpec(memory_space=pl.ANY),
             pl.BlockSpec(memory_space=pltpu.VMEM),
         ],
         out_specs=pl.BlockSpec(memory_space=pltpu.VMEM),
-        scratch_shapes=[
-            pltpu.VMEM((slots * window, width), jnp.bfloat16),
-            pltpu.SemaphoreType.DMA,
-        ],
+        scratch_shapes=[pltpu.VMEM((remote, width), jnp.bfloat16), pltpu.SemaphoreType.DMA],
         compiler_params=pltpu.CompilerParams(vmem_limit_bytes=16 * 1024 * 1024),
         cost_estimate=pl.CostEstimate(
             flops=8 * slots * window * rows * width, bytes_accessed=6 * rows * width, transcendentals=0
         ),
         name="contract",
-    )(heads, pltpu.with_memory_space_constraint(tails, pltpu.HBM), arrived.reshape(rows * depth, LANES))
+    )(
+        member.astype(jnp.int32)[None],
+        heads,
+        pltpu.with_memory_space_constraint(tails, pltpu.HBM),
+        arrived.reshape(rows * depth, LANES),
+    )
 
     mine = pl.pallas_call(
         contract_own,
@@ -140,7 +148,7 @@
 
     groups = [[i + stride * k for k in range(slots)] for i in range(stride)]
     moved = lax.all_to_all(
-        terms.reshape(slots, window, rows), "vv", split_axis=0, concat_axis=0, axis_index_groups=groups, tiled=True
+        terms, "vv", split_axis=0, concat_axis=0, axis_index_groups=groups, tiled=True
     )
     total = ((moved[0] + moved[1]) + (moved[2] + moved[3])) + mine
     return total.reshape(1, window, 1, rows)

time: 86.3 us -> 86.2 us (level)
  no operation moved by 1% of the time
where the time goes in v6:
time: 86.2 us; the launch traced here: 85.7 us
  waiting for transfers between devices  53.7 us (62%)
  starting transfers between devices  21.3 us (25%)
  Pallas kernels  6.51 us (8%)
  local copies, waits for them, and re-layouts  2.83 us (3%)
    all_to_all x1, waiting for transfers between devices, shards(): lax.all_to_all(amplitudes.reshape(rows, depth, LANES), 'vv', split_axis=0...  47.3 us
    all_to_all x1, starting transfers between devices, shards(): lax.all_to_all(amplitudes.reshape(rows, depth, LANES), 'vv', split_axis=0...  17.9 us
    all_to_all x1, waiting for transfers between devices, shards(): lax.all_to_all(terms, 'vv', split_axis=0, concat_axis=0, axis_index_group...  6.37 us
    all_to_all x1, starting transfers between devices, shards(): lax.all_to_all(terms, 'vv', split_axis=0, concat_axis=0, axis_index_group...  3.37 us
    pallas_call x1, Pallas kernels, shards(): pl.pallas_call(contract, out_shape=pltpu.VMEM((slots, window, rows), jnp....  2.91 us
    unnamed x8, local copies, waits for them, and re-layouts  2.83 us
    pallas_call x1, Pallas kernels, shards(): pl.pallas_call(split_blocks, out_shape=[jax.ShapeDtypeStruct((remote, wid...  2.14 us
  transfers between devices with their start and end apart: 2, of which 2 were waited for; matrix products, arithmetic and copies ran while one was open for 0% of the time, Pallas kernels for 4%

profile of v6, /device:TPU:6, one launch (start us, length us, event | category | flops | bytes accessed | tf_op | source)
XLA Modules:
  0.0 85.7 jit_solution(1487672288075812177)
XLA Ops:
  0.0 0.0 copy-start.2
  0.0 0.0 copy-start.3
  0.0 17.9 %all-to-all-start = ((f32[128,32,128]{2,1,0:T(8,128)}), f32[128,32,128]{2,1,0:T(8,128)S(1)}, u32[]{:S(2)}, u32[]{:S(2)}) async-start(f32[128,32,128]{2,1,0:T(8,128)} %bitcast.14), calls=%async_computation | async-start | bytes 4194304 | tf_op jit(solution)/shard_map/all_to_all | solution.py:92
  18.6 0.0 copy-done.2
  18.6 0.0 copy-done.3
  18.6 0.0 copy-start
  18.6 1.7 %copy-done = f32[1,4,40,4096]{3,2,1,0:T(8,128)S(1)} copy-done((f32[1,4,40,4096]{3,2,1,0:T(8,128)S(1)}, f32[1,4,40,4096]{3,2,1,0:T(8,128)}, u32[]{:S(2)}) %copy-start) | copy-done | bytes 2621464
  20.4 2.1 %split_blocks.1 = (bf16[128,4096]{1,0:T(8,128)(2,1)S(1)}, bf16[128,4096]{1,0:T(8,128)(2,1)}, bf16[80,4096]{1,0:T(8,128)(2,1)}) custom-call(s32[16]{0:T(128)S(1)} %copy-done.2, s32[1,2]{1,0:T(1,128)S(1)} %copy-done.3, s32[1]{0:T(128)S(6)} %copy.7.count_ref, f32[4,40,4096]{2,1,0:T(8,128)S(1)} %bitcast.13), custom_call_target="tpu_custom_call" | custom-call | flops 5242880 | bytes 5242880 | tf_op jit(solution)/shard_map/split_blocks/pallas_call | solution.py:98
  22.5 47.3 %all-to-all-done = f32[128,32,128]{2,1,0:T(8,128)S(1)} async-done(((f32[128,32,128]{2,1,0:T(8,128)}), f32[128,32,128]{2,1,0:T(8,128)S(1)}, u32[]{:S(2)}, u32[]{:S(2)}) %all-to-all-start) | async-done | bytes 2097184 | tf_op jit(solution)/shard_map/all_to_all | solution.py:92
  69.9 2.9 %contract.1 = f32[4,40,128]{2,1,0:T(8,128)} custom-call(s32[1]{0:T(128)} %bitcast.member_ref, bf16[128,4096]{1,0:T(8,128)(2,1)S(1)} %get-tuple-element.8.head_ref, bf16[128,4096]{1,0:T(8,128)(2,1)} %get-tuple-element.9.tail_hbm, f32[4096,128]{1,0:T(8,128)S(1)} %bitcast.11), custom_call_target="tpu_custom_call" | custom-call | flops 671088640 | bytes 3145728 | tf_op jit(solution)/shard_map/contract/pallas_call | solution.py:114
  72.8 3.4 %all-to-all-start.1 = ((f32[4,40,128]{2,1,0:T(8,128)}), f32[4,40,128]{2,1,0:T(8,128)S(1)}, u32[]{:S(2)}, u32[]{:S(2)}) async-start(f32[4,40,128]{2,1,0:T(8,128)} %contract.1), calls=%async_computation.1 | async-start | bytes 163840 | tf_op jit(solution)/shard_map/all_to_all | solution.py:150
  76.1 0.0 copy-start.1
  76.2 1.1 %copy-done.1 = bf16[80,4096]{1,0:T(8,128)(2,1)S(1)} copy-done((bf16[80,4096]{1,0:T(8,128)(2,1)S(1)}, bf16[80,4096]{1,0:T(8,128)(2,1)}, u32[]{:S(2)}) %copy-start.1) | copy-done | bytes 655384
  77.2 1.5 %contract_own.1 = f32[40,128]{1,0:T(8,128)S(1)} custom-call(bf16[80,4096]{1,0:T(8,128)(2,1)S(1)} %copy-done.1, f32[4096,128]{1,0:T(8,128)S(1)} %bitcast.12), custom_call_target="tpu_custom_call" | custom-call | flops 671088640 | bytes 3145728 | tf_op jit(solution)/shard_map/contract_own/pallas_call | solution.py:137
  78.7 6.4 %all-to-all-done.1 = f32[4,40,128]{2,1,0:T(8,128)S(1)} async-done(((f32[4,40,128]{2,1,0:T(8,128)}), f32[4,40,128]{2,1,0:T(8,128)S(1)}, u32[]{:S(2)}, u32[]{:S(2)}) %all-to-all-start.1) | async-done | bytes 81952 | tf_op jit(solution)/shard_map/all_to_all | solution.py:150
  85.1 0.6 fusion.2
Async XLA Ops:
  0.0 18.6 %copy-start.2 = (s32[16]{0:T(128)S(1)}, s32[16]{0:T(128)}, u32[]{:S(2)}) copy-start(s32[16]{0:T(128)} %tile_len_ref.1) | copy-start | bytes 196
  0.0 18.6 %copy-start.3 = (s32[1,2]{1,0:T(1,128)S(1)}, s32[1,2]{1,0:T(1,128)}, u32[]{:S(2)}) copy-start(s32[1,2]{1,0:T(1,128)} %pair_ref.1) | copy-start | bytes 28
  0.0 69.9 %all-to-all-start = ((f32[128,32,128]{2,1,0:T(8,128)}), f32[128,32,128]{2,1,0:T(8,128)S(1)}, u32[]{:S(2)}, u32[]{:S(2)}) async-start(f32[128,32,128]{2,1,0:T(8,128)} %bitcast.14), calls=%async_computation | async-start | bytes 4194304 | tf_op jit(solution)/shard_map/all_to_all | solution.py:92
  18.6 1.7 %copy-start = (f32[1,4,40,4096]{3,2,1,0:T(8,128)S(1)}, f32[1,4,40,4096]{3,2,1,0:T(8,128)}, u32[]{:S(2)}) copy-start(f32[1,4,40,4096]{3,2,1,0:T(8,128)} %param.8) | copy-start | bytes 7864324
  72.8 12.3 %all-to-all-start.1 = ((f32[4,40,128]{2,1,0:T(8,128)}), f32[4,40,128]{2,1,0:T(8,128)S(1)}, u32[]{:S(2)}, u32[]{:S(2)}) async-start(f32[4,40,128]{2,1,0:T(8,128)} %contract.1), calls=%async_computation.1 | async-start | bytes 163840 | tf_op jit(solution)/shard_map/all_to_all | solution.py:150
  76.1 1.1 %copy-start.1 = (bf16[80,4096]{1,0:T(8,128)(2,1)S(1)}, bf16[80,4096]{1,0:T(8,128)(2,1)}, u32[]{:S(2)}) copy-start(bf16[80,4096]{1,0:T(8,128)(2,1)} %get-tuple-element.10.own_ref) | copy-start | bytes 1966084

commit v7 on v3

--- a/solution.py
+++ b/solution.py
@@ -7,7 +7,7 @@
 
 TV = 64
 LANES = 128
-CHUNKS = 2
+FIRST = 11 / 16
 
 
 def split_blocks(tile_len_ref, pair_ref, count_ref, member_ref, v_ref, head_ref, tail_ref):
@@ -41,18 +41,18 @@
     copy.start()
     half, rows = out_ref.shape
     depth = amp_ref.shape[0] // rows
-    chunk = depth // CHUNKS
+    cut = int(depth * FIRST)
     both = None
-    for start in range(0, depth, chunk):
+    for start, end in ((0, cut), (cut, depth)):
         heads, tails = [], []
-        for j in range(start, start + chunk):
+        for j in range(start, end):
             part = amp_ref[pl.ds(j, rows, stride=depth), :]
             heads.append(part.astype(jnp.bfloat16))
             tails.append((part - heads[-1].astype(jnp.float32)).astype(jnp.bfloat16))
         amp = jnp.concatenate([jnp.concatenate(heads, axis=1), jnp.concatenate(tails, axis=1)], axis=0)
         if start == 0:
             copy.wait()
-        lanes = pl.ds(start * LANES, chunk * LANES)
+        lanes = pl.ds(start * LANES, (end - start) * LANES)
         blocks = jnp.concatenate([head_ref[:, lanes], tail_ref[:, lanes]], axis=0)
         product = times_transposed(blocks, amp)
         both = product if both is None else both + product

time: 85.4 us -> 85.2 us (level)
  no operation moved by 1% of the time
where the time goes in v7:
time: 85.2 us; the launch traced here: 85 us
  waiting for transfers between devices  47.5 us (56%)
  starting transfers between devices  17.9 us (21%)
  blocking collectives  12.1 us (14%)
  Pallas kernels  4.4 us (5%)
  local copies, waits for them, and re-layouts  1.74 us (2%)
    all_to_all x1, waiting for transfers between devices, shards(): lax.all_to_all(amplitudes.reshape(rows, depth, LANES), 'vv', split_axis=0...  47.5 us
    all_to_all x1, starting transfers between devices, shards(): lax.all_to_all(amplitudes.reshape(rows, depth, LANES), 'vv', split_axis=0...  17.9 us
    all_to_all x1, blocking collectives, shards(): lax.all_to_all(terms.reshape(slots, window, rows), 'vv', split_axis=0, co...  12.1 us
    pallas_call x1, Pallas kernels, shards(): pl.pallas_call(contract, out_shape=jax.ShapeDtypeStruct((slots * window,...  2.41 us
    pallas_call x1, Pallas kernels, shards(): pl.pallas_call(split_blocks, out_shape=[jax.ShapeDtypeStruct((slots * win...  1.99 us
    unnamed x6, local copies, waits for them, and re-layouts  1.74 us
  transfers between devices with their start and end apart: 1, of which 1 were waited for; matrix products, arithmetic and copies ran while one was open for 0% of the time, Pallas kernels for 2%

profile of v7, /device:TPU:6, one launch (start us, length us, event | category | flops | bytes accessed | tf_op | source)
XLA Modules:
  0.0 85.0 jit_solution(2025665839451868083)
XLA Ops:
  0.0 0.0 copy-start.1
  0.0 0.0 copy-start.2
  0.0 17.9 %all-to-all-start = ((f32[128,32,128]{2,1,0:T(8,128)}), f32[128,32,128]{2,1,0:T(8,128)S(1)}, u32[]{:S(2)}, u32[]{:S(2)}) async-start(f32[128,32,128]{2,1,0:T(8,128)} %bitcast.9), calls=%async_computation | async-start | bytes 4194304 | tf_op jit(solution)/shard_map/all_to_all | solution.py:68
  18.6 0.0 copy-done.1
  18.6 0.0 copy-done.2
  18.6 0.0 copy-start
  18.6 1.7 %copy-done = f32[1,4,40,4096]{3,2,1,0:T(8,128)S(1)} copy-done((f32[1,4,40,4096]{3,2,1,0:T(8,128)S(1)}, f32[1,4,40,4096]{3,2,1,0:T(8,128)}, u32[]{:S(2)}) %copy-start) | copy-done | bytes 2621464
  20.4 2.0 %split_blocks.1 = (bf16[160,4096]{1,0:T(8,128)(2,1)S(1)}, bf16[160,4096]{1,0:T(8,128)(2,1)}) custom-call(s32[16]{0:T(128)S(1)} %copy-done.1, s32[1,2]{1,0:T(1,128)S(1)} %copy-done.2, s32[1]{0:T(128)S(6)} %copy.6.count_ref, s32[1]{0:T(128)} %bitcast.member_ref, f32[4,40,4096]{2,1,0:T(8,128)S(1)} %bitcast.7), custom_call_target="tpu_custom_call" | custom-call | flops 5242880 | bytes 5242880 | tf_op jit(solution)/shard_map/split_blocks/pallas_call | solution.py:73
  22.4 47.5 %all-to-all-done = f32[128,32,128]{2,1,0:T(8,128)S(1)} async-done(((f32[128,32,128]{2,1,0:T(8,128)}), f32[128,32,128]{2,1,0:T(8,128)S(1)}, u32[]{:S(2)}, u32[]{:S(2)}) %all-to-all-start) | async-done | bytes 2097184 | tf_op jit(solution)/shard_map/all_to_all | solution.py:68
  69.9 2.4 %contract.1 = f32[160,128]{1,0:T(8,128)S(1)} custom-call(bf16[160,4096]{1,0:T(8,128)(2,1)S(1)} %get-tuple-element.7.head_ref, bf16[160,4096]{1,0:T(8,128)(2,1)} %get-tuple-element.8.tail_hbm, f32[4096,128]{1,0:T(8,128)S(1)} %bitcast.6), custom_call_target="tpu_custom_call" | custom-call | flops 671088640 | bytes 3145728 | tf_op jit(solution)/shard_map/contract/pallas_call | solution.py:88
  72.3 12.1 %all_to_all.10 = f32[4,40,128]{2,1,0:T(8,128)S(1)} all-to-all(f32[4,40,128]{2,1,0:T(8,128)S(1)} %bitcast.8), channel_id=1, replica_groups={{0,128,256,384},{4,132,260,388},{8,136,264,392},{12,140,268,396},{16,14..., dimensions={0} | all-to-all | bytes 163840 | tf_op jit(solution)/shard_map/all_to_all | solution.py:109
  84.4 0.6 fusion
Async XLA Ops:
  0.0 18.6 %copy-start.1 = (s32[16]{0:T(128)S(1)}, s32[16]{0:T(128)}, u32[]{:S(2)}) copy-start(s32[16]{0:T(128)} %tile_len_ref.1) | copy-start | bytes 196
  0.0 18.6 %copy-start.2 = (s32[1,2]{1,0:T(1,128)S(1)}, s32[1,2]{1,0:T(1,128)}, u32[]{:S(2)}) copy-start(s32[1,2]{1,0:T(1,128)} %pair_ref.1) | copy-start | bytes 28
  0.0 69.9 %all-to-all-start = ((f32[128,32,128]{2,1,0:T(8,128)}), f32[128,32,128]{2,1,0:T(8,128)S(1)}, u32[]{:S(2)}, u32[]{:S(2)}) async-start(f32[128,32,128]{2,1,0:T(8,128)} %bitcast.9), calls=%async_computation | async-start | bytes 4194304 | tf_op jit(solution)/shard_map/all_to_all | solution.py:68
  18.6 1.7 %copy-start = (f32[1,4,40,4096]{3,2,1,0:T(8,128)S(1)}, f32[1,4,40,4096]{3,2,1,0:T(8,128)}, u32[]{:S(2)}) copy-start(f32[1,4,40,4096]{3,2,1,0:T(8,128)} %param.8) | copy-start | bytes 7864324

commit v8 on v7

--- a/solution.py
+++ b/solution.py
@@ -7,7 +7,7 @@
 
 TV = 64
 LANES = 128
-FIRST = 11 / 16
+FIRST = 13 / 16
 
 
 def split_blocks(tile_len_ref, pair_ref, count_ref, member_ref, v_ref, head_ref, tail_ref):

time: 85.2 us -> 85.4 us (level)
  no operation moved by 1% of the time
where the time goes in v8:
time: 85.4 us; the launch traced here: 85.2 us
  waiting for transfers between devices  47.5 us (56%)
  starting transfers between devices  17.9 us (21%)
  blocking collectives  12.1 us (14%)
  Pallas kernels  4.58 us (5%)
  local copies, waits for them, and re-layouts  1.74 us (2%)
    all_to_all x1, waiting for transfers between devices, shards(): lax.all_to_all(amplitudes.reshape(rows, depth, LANES), 'vv', split_axis=0...  47.5 us
    all_to_all x1, starting transfers between devices, shards(): lax.all_to_all(amplitudes.reshape(rows, depth, LANES), 'vv', split_axis=0...  17.9 us
    all_to_all x1, blocking collectives, shards(): lax.all_to_all(terms.reshape(slots, window, rows), 'vv', split_axis=0, co...  12.1 us
    pallas_call x1, Pallas kernels, shards(): pl.pallas_call(contract, out_shape=jax.ShapeDtypeStruct((slots * window,...  2.59 us
    pallas_call x1, Pallas kernels, shards(): pl.pallas_call(split_blocks, out_shape=[jax.ShapeDtypeStruct((slots * win...  1.99 us
    unnamed x6, local copies, waits for them, and re-layouts  1.74 us
  transfers between devices with their start and end apart: 1, of which 1 were waited for; matrix products, arithmetic and copies ran while one was open for 0% of the time, Pallas kernels for 2%

profile of v8, /device:TPU:6, one launch (start us, length us, event | category | flops | bytes accessed | tf_op | source)
XLA Modules:
  0.0 85.2 jit_solution(9484732269757763623)
XLA Ops:
  0.0 0.0 copy-start.1
  0.0 0.0 copy-start.2
  0.0 17.9 %all-to-all-start = ((f32[128,32,128]{2,1,0:T(8,128)}), f32[128,32,128]{2,1,0:T(8,128)S(1)}, u32[]{:S(2)}, u32[]{:S(2)}) async-start(f32[128,32,128]{2,1,0:T(8,128)} %bitcast.9), calls=%async_computation | async-start | bytes 4194304 | tf_op jit(solution)/shard_map/all_to_all | solution.py:68
  18.6 0.0 copy-done.1
  18.6 0.0 copy-done.2
  18.6 0.0 copy-start
  18.6 1.7 %copy-done = f32[1,4,40,4096]{3,2,1,0:T(8,128)S(1)} copy-done((f32[1,4,40,4096]{3,2,1,0:T(8,128)S(1)}, f32[1,4,40,4096]{3,2,1,0:T(8,128)}, u32[]{:S(2)}) %copy-start) | copy-done | bytes 2621464
  20.4 2.0 %split_blocks.1 = (bf16[160,4096]{1,0:T(8,128)(2,1)S(1)}, bf16[160,4096]{1,0:T(8,128)(2,1)}) custom-call(s32[16]{0:T(128)S(1)} %copy-done.1, s32[1,2]{1,0:T(1,128)S(1)} %copy-done.2, s32[1]{0:T(128)S(6)} %copy.6.count_ref, s32[1]{0:T(128)} %bitcast.member_ref, f32[4,40,4096]{2,1,0:T(8,128)S(1)} %bitcast.7), custom_call_target="tpu_custom_call" | custom-call | flops 5242880 | bytes 5242880 | tf_op jit(solution)/shard_map/split_blocks/pallas_call | solution.py:73
  22.4 47.5 %all-to-all-done = f32[128,32,128]{2,1,0:T(8,128)S(1)} async-done(((f32[128,32,128]{2,1,0:T(8,128)}), f32[128,32,128]{2,1,0:T(8,128)S(1)}, u32[]{:S(2)}, u32[]{:S(2)}) %all-to-all-start) | async-done | bytes 2097184 | tf_op jit(solution)/shard_map/all_to_all | solution.py:68
  69.9 2.6 %contract.1 = f32[160,128]{1,0:T(8,128)S(1)} custom-call(bf16[160,4096]{1,0:T(8,128)(2,1)S(1)} %get-tuple-element.7.head_ref, bf16[160,4096]{1,0:T(8,128)(2,1)} %get-tuple-element.8.tail_hbm, f32[4096,128]{1,0:T(8,128)S(1)} %bitcast.6), custom_call_target="tpu_custom_call" | custom-call | flops 671088640 | bytes 3145728 | tf_op jit(solution)/shard_map/contract/pallas_call | solution.py:88
  72.5 12.1 %all_to_all.10 = f32[4,40,128]{2,1,0:T(8,128)S(1)} all-to-all(f32[4,40,128]{2,1,0:T(8,128)S(1)} %bitcast.8), channel_id=1, replica_groups={{0,128,256,384},{4,132,260,388},{8,136,264,392},{12,140,268,396},{16,14..., dimensions={0} | all-to-all | bytes 163840 | tf_op jit(solution)/shard_map/all_to_all | solution.py:109
  84.5 0.6 fusion
Async XLA Ops:
  0.0 18.6 %copy-start.1 = (s32[16]{0:T(128)S(1)}, s32[16]{0:T(128)}, u32[]{:S(2)}) copy-start(s32[16]{0:T(128)} %tile_len_ref.1) | copy-start | bytes 196
  0.0 18.6 %copy-start.2 = (s32[1,2]{1,0:T(1,128)S(1)}, s32[1,2]{1,0:T(1,128)}, u32[]{:S(2)}) copy-start(s32[1,2]{1,0:T(1,128)} %pair_ref.1) | copy-start | bytes 28
  0.0 69.9 %all-to-all-start = ((f32[128,32,128]{2,1,0:T(8,128)}), f32[128,32,128]{2,1,0:T(8,128)S(1)}, u32[]{:S(2)}, u32[]{:S(2)}) async-start(f32[128,32,128]{2,1,0:T(8,128)} %bitcast.9), calls=%async_computation | async-start | bytes 4194304 | tf_op jit(solution)/shard_map/all_to_all | solution.py:68
  18.6 1.7 %copy-start = (f32[1,4,40,4096]{3,2,1,0:T(8,128)S(1)}, f32[1,4,40,4096]{3,2,1,0:T(8,128)}, u32[]{:S(2)}) copy-start(f32[1,4,40,4096]{3,2,1,0:T(8,128)} %param.8) | copy-start | bytes 7864324
